TPU v7x, 32 devices: a whole 2x2x4 slice. The times are simulated.
32 devices in a mesh: fsdp: 2 (over x), blk: 16 (over z, y, core).
Axes of the slice: x: 2, y: 2, z: 4, core: 2. Of those that a mesh axis runs over, the one named last changes fastest.
Arguments:
- question_activations: bfloat16 [64, 64, 768], P(('fsdp', 'blk')), may hold values from -6 to 6
- passage_activations: bfloat16 [64, 768, 768], P(('fsdp', 'blk')), may hold values from -6 to 6
- question_unpadded_counts: int32 [64], P(('fsdp', 'blk')), may hold values from 8 to 64, as said below
- passage_unpadded_counts: int32 [64], P(('fsdp', 'blk')), may hold values from 96 to 768, as said below
- correct_passage_index: int32 [64], P(('fsdp', 'blk')), may hold values from 0 to 63, each once
- query_weights: float32 [64], P(('fsdp', 'blk')), may hold values from 0.5 to 8.4
- softness_factor: float32 [1], replicated, may hold values from 0.1 to 0.2
- combined_projection_matrix: bfloat16 [768, 2304], P('fsdp'), may hold values from -0.21875 to 0.21875
- mixing_result_matrix: bfloat16 [768, 768], P('fsdp'), may hold values from -0.875 to 0.875
- gating_matrix: bfloat16 [768, 3072], P('fsdp'), may hold values from -0.21875 to 0.21875
- widening_matrix: bfloat16 [768, 3072], P('fsdp'), may hold values from -0.21875 to 0.21875
- narrowing_matrix: bfloat16 [3072, 768], P('fsdp'), may hold values from -0.109375 to 0.109375
- initial_layernorm_scale: bfloat16 [768], P('fsdp'), may hold values from 0.5 to 1.5
- initial_layernorm_shift: bfloat16 [768], P('fsdp'), may hold values from -0.59765625 to 0.59765625
- later_layernorm_scale: bfloat16 [768], P('fsdp'), may hold values from 0.5 to 1.5
- later_layernorm_shift: bfloat16 [768], P('fsdp'), may hold values from -0.59765625 to 0.59765625
Outputs:
- loss: float32 [1], replicated
- grad_queries: float32 [64, 64, 768], P(('fsdp', 'blk'))
- grad_documents: float32 [64, 768, 768], P(('fsdp', 'blk'))
- grad_qkv: float32 [768, 2304], P('fsdp')
- grad_out: float32 [768, 768], P('fsdp')
- grad_gate: float32 [768, 3072], P('fsdp')
- grad_up: float32 [768, 3072], P('fsdp')
- grad_down: float32 [3072, 768], P('fsdp')
- grad_norm1_gain: float32 [768], P('fsdp')
- grad_norm1_bias: float32 [768], P('fsdp')
- grad_norm2_gain: float32 [768], P('fsdp')
- grad_norm2_bias: float32 [768], P('fsdp')
Inputs may be any that keep to these rules, and one draw needn't show every extreme that they name: `question_unpadded_counts`: some query has exactly 64 tokens and some exactly 8. `passage_unpadded_counts`: some document has exactly 768 tokens and some exactly 96. `correct_passage_index`: each document index appears once.
All inputs are finite; a program needn't handle non-finite values.
Results may differ from a plain program's by a relative error of at most 0.028.
Values may be sent and summed in bfloat16 or wider, within the bound.
No kernel may reach another device: no remote copies, remote signals or barrier semaphores. Data moves between devices by JAX's collectives and lax.ppermute only.
A program may use at most 320 MiB of HBM per device.

v0:
```python
import functools

import jax
import jax.numpy as jnp
import numpy as np
from jax import lax
from jax.experimental import pallas as pl
from jax.experimental.pallas import tpu as pltpu
from jax.sharding import PartitionSpec as P

HEAD = 64
BLOCK = 128
TILE = 256
EPS_NORM = 1e-05
EPS_UNIT = 1e-06
MASKED = -1e30
F32 = jnp.float32
BF16 = jnp.bfloat16
PACE = 0.5
SPAN = 512
OFF0, OFF1, OFFQ, LEN0, LEN1, QLEN0, QLEN1, CNT0, CNT1, TILES, CORE, SIDE, ROW, SLOT, STAY, IDS = range(16)


def dot(left, right, contract=((1,), (0,))):
    return lax.dot_general(left, right, (contract, ((), ())), preferred_element_type=F32)


def cost(microseconds):
    return pl.CostEstimate(flops=int(microseconds * PACE * 1e9), bytes_accessed=0, transcendentals=0)


def params(mebibytes=60):
    return pltpu.CompilerParams(vmem_limit_bytes=mebibytes * 1024 * 1024)


def rotary_tables(doc_len, query_len):
    frequency = 1000.0 ** (-(np.arange(HEAD // 2, dtype=np.float32) * 2.0 / HEAD))
    positions = np.concatenate([np.arange(doc_len), np.arange(query_len), np.arange(query_len)])
    angles = positions.astype(np.float32)[:, None] * frequency.astype(np.float32)[None, :]
    cosine, sine = np.cos(angles), np.sin(angles)
    return (
        np.concatenate([cosine] * 4, axis=1).astype(np.float32),
        np.concatenate([-sine, sine, -sine, sine], axis=1).astype(np.float32),
    )


def swap_halves(pair):
    lane = lax.broadcasted_iota(jnp.int32, pair.shape, 1)
    return jnp.where(lane % HEAD < HEAD // 2, pltpu.roll(pair, 96, 1), pltpu.roll(pair, 32, 1))


def live(step, meta):
    return jnp.minimum(step, meta[TILES] - 1)


def tiled(columns, at=0):
    return pl.BlockSpec((TILE, columns), lambda i, m, *_: (live(i, m), at))


def while_live(kernel):
    @functools.wraps(kernel)
    def run(meta, *refs):
        @pl.when(pl.program_id(0) < meta[TILES])
        def _():
            kernel(meta, *refs)

    return run


def anywhere(count):
    return [pl.BlockSpec(memory_space=pl.ANY)] * count


def resident(shape):
    return pl.BlockSpec(shape, lambda *_: (0,) * len(shape), pipeline_mode=pl.Buffered(1))


def piece_copies(meta, rows, pieces, whole, sems):
    side, row, core = meta[SIDE], meta[ROW], meta[CORE]
    parts = len(pieces) - 1
    if parts == 2:
        places = [core, 1 - core]
    else:
        places = [row * 2 + core, (1 - row) * 2 + core, row * 2 + 1 - core, (1 - row) * 2 + 1 - core]
    size = rows // parts
    starts = [side * rows] + [(1 - side) * rows + place * size for place in places]
    return [
        pltpu.make_async_copy(
            piece, whole.at[pl.ds(pl.multiple_of(start, 16), piece.shape[0]), :], sems.at[at]
        )
        for at, (piece, start) in enumerate(zip(pieces, starts))
    ]


def qkv_kernel(meta, table_block, x_ref, cos_ref, sin_ref, *refs):
    pieces, (out_ref, turned_out, w_ref, turned, sems, out_sem) = refs[:3], refs[-6:]
    tile = pl.program_id(0)
    keep = pltpu.make_async_copy(turned, turned_out, out_sem)

    @pl.when(tile == 0)
    def _():
        copies = piece_copies(meta, pieces[0].shape[0], pieces, w_ref, sems)
        for copy in copies:
            copy.start()
        for copy in copies:
            copy.wait()

    @pl.when(tile == 1)
    def _():
        width = x_ref.shape[1]
        for pair in range(width // 128):
            for part in range(3):
                at, to = part * width + pair * 128, (pair * 3 + part) * 128
                turned[to : to + 128, :] = w_ref[:, at : at + 128].T
        keep.start()

    @pl.when(tile < meta[TILES])
    def _():
        x = x_ref[...]
        width = x.shape[1]

        def turn(part, acc):
            scale = HEAD**-0.5 if part == 0 else 1.0
            for sub in range(TILE // BLOCK):
                rows = slice(sub * BLOCK, (sub + 1) * BLOCK)
                table = pl.ds(table_block[tile * (TILE // BLOCK) + sub] * BLOCK, BLOCK)
                cosine, sine = cos_ref[table, :] * scale, sin_ref[table, :] * scale
                for group in range(width // 128):
                    pair = acc[rows, group * 128 : (group + 1) * 128]
                    turned_pair = pair * cosine + swap_halves(pair) * sine
                    at = part * width + group * 128
                    out_ref[rows, at : at + 128] = turned_pair.astype(BF16)

        queries = dot(x, w_ref[:, :width])
        keys = dot(x, w_ref[:, width : 2 * width])
        turn(0, queries)
        values = dot(x, w_ref[:, 2 * width :])
        turn(1, keys)
        out_ref[:, 2 * width :] = values.astype(BF16)

    @pl.when(tile == pl.num_programs(0) - 1)
    def _():
        keep.wait()


def project(meta, table_block, x, pieces, tables, after=()):
    rows, width = x.shape
    whole = (width, 3 * width)
    grid_spec = pltpu.PrefetchScalarGridSpec(
        num_scalar_prefetch=2,
        grid=(rows // TILE,),
        in_specs=[tiled(width), resident(tables[0].shape), resident(tables[1].shape)]
        + anywhere(len(pieces) + len(after)),
        out_specs=[tiled(3 * width)] + anywhere(1),
        scratch_shapes=[
            pltpu.VMEM(whole, BF16),
            pltpu.VMEM(whole[::-1], BF16),
            pltpu.SemaphoreType.DMA((len(pieces),)),
            pltpu.SemaphoreType.DMA,
        ],
    )
    return pl.pallas_call(
        qkv_kernel,
        grid_spec=grid_spec,
        out_shape=[
            jax.ShapeDtypeStruct((rows, 3 * width), BF16),
            jax.ShapeDtypeStruct(whole[::-1], BF16),
        ],
        compiler_params=params(36),
        cost_estimate=cost(11),
        name="qkv",
    )(meta, table_block, x, *tables, *pieces, *after)


def split_pair(pair):
    lane = lax.broadcasted_iota(jnp.int32, pair.shape, 1)
    zero = jnp.zeros_like(pair)
    return jnp.concatenate(
        [jnp.where(lane < HEAD, pair, zero), jnp.where(lane < HEAD, zero, pair)], axis=0
    )


def mask_keys(scores, last, valid):
    rows = lax.broadcasted_iota(jnp.int32, (BLOCK, scores.shape[1]), 0)
    tail = jnp.where(rows < valid, scores[last * BLOCK :, :], MASKED)
    if last == 0:
        return tail
    return jnp.concatenate([scores[: last * BLOCK, :], tail], axis=0)


def query_mask(meta, scores):
    half = scores.shape[0] // 2
    key = lax.broadcasted_iota(jnp.int32, scores.shape, 0)
    row = lax.broadcasted_iota(jnp.int32, scores.shape, 1) % (2 * half)
    length = jnp.where(key < half, meta[QLEN0], meta[QLEN1])
    keep = ((key < half) == (row < half)) & (key % half < length)
    return jnp.where(keep, scores, MASKED)


def split_turned(pair):
    turned = pair.T
    row = lax.broadcasted_iota(jnp.int32, turned.shape, 0)
    zero = jnp.zeros_like(turned)
    return jnp.concatenate(
        [jnp.where(row < HEAD, turned, zero), jnp.where(row < HEAD, zero, turned)], axis=1
    )


def stack_heads(pair_wide):
    half = pair_wide.shape[1] // 2
    return jnp.concatenate([pair_wide[:, :half], pair_wide[:, half:]], axis=0)


def attend_kernel(meta, q_ref, k_ref, v_ref, *refs):
    out_ref, lse_ref = refs[-2:]

    def scores_of(start, size, keys, masked):
        return masked(dot(keys, split_pair(q_ref[pl.ds(start, size), :]), ((1,), (1,))))

    def finish(start, size, scores, values):
        rows = pl.ds(start, size)
        highest = jnp.max(scores, axis=0, keepdims=True)
        exponent = jnp.exp(scores - highest)
        total = jnp.sum(exponent, axis=0, keepdims=True)
        attended = dot(values, stack_heads(exponent.astype(BF16)))
        recip = 1.0 / total
        row = lax.broadcasted_iota(jnp.int32, attended.shape, 0)
        attended = attended * jnp.where(row < HEAD, recip[:, :size], recip[:, size:])
        out_ref[rows, :] = attended.T.astype(BF16)
        log_norm = highest + jnp.log(total)
        lse_ref[0, 0:1, rows] = log_norm[:, :size]
        lse_ref[0, 1:2, rows] = log_norm[:, size:]

    def run(starts, size, keys, values, masked):
        ahead = scores_of(starts[0], size, keys, masked)
        for at, start in enumerate(starts):
            scores = ahead
            if at + 1 < len(starts):
                ahead = scores_of(starts[at + 1], size, keys, masked)
            finish(start, size, scores, values)

    @pl.loop(0, 2)
    def _(doc):
        start = pl.multiple_of(meta[OFF0 + doc], BLOCK)
        for blocks in range(1, 7):

            @pl.when(meta[CNT0 + doc] == blocks)
            def _():
                whole = pl.ds(start, blocks * BLOCK)
                valid = meta[LEN0 + doc] - (blocks - 1) * BLOCK
                starts = [pl.multiple_of(start + at * TILE, BLOCK) for at in range((blocks + 1) // 2)]
                run(
                    starts, TILE, k_ref[whole, :], split_turned(v_ref[whole, :]),
                    lambda scores: mask_keys(scores, blocks - 1, valid),
                )

    first = pl.multiple_of(meta[OFFQ], BLOCK)
    rows = pl.ds(first, BLOCK)
    run(
        [first], BLOCK, k_ref[rows, :], split_turned(v_ref[rows, :]), functools.partial(query_mask, meta)
    )
    out_ref[pl.ds(first + BLOCK, BLOCK), :] = jnp.zeros((BLOCK, 128), BF16)


def attend(meta, qkv, group, members, before=(), after=()):
    rows, width = qkv.shape[0], qkv.shape[1] // 3
    pairs = width // 128

    def column(part):
        return pl.BlockSpec((rows, 128), lambda h, *_: (0, part * pairs + group * members + h))

    grid_spec = pltpu.PrefetchScalarGridSpec(
        num_scalar_prefetch=1,
        grid=(members,),
        in_specs=[column(0), column(1), column(2)] + anywhere(len(before) + len(after)),
        out_specs=[
            column(0),
            pl.BlockSpec((1, 8, rows), lambda h, *_: (group * members + h, 0, 0)),
        ],
    )
    return pl.pallas_call(
        attend_kernel,
        grid_spec=grid_spec,
        out_shape=[
            jax.ShapeDtypeStruct((rows, width), BF16),
            jax.ShapeDtypeStruct((pairs, 8, rows), F32),
        ],
        input_output_aliases={4 + at: at for at in range(len(before))},
        compiler_params=params(28),
        cost_estimate=cost(13),
        name="attend",
    )(meta, qkv, qkv, qkv, *before, *after)


def normalize(summed):
    centered = summed - jnp.mean(summed, axis=-1, keepdims=True)
    recip = lax.rsqrt(jnp.mean(centered * centered, axis=-1, keepdims=True) + EPS_NORM)
    return centered * recip, recip


def forward_kernel(
    meta, counts, att_ref, x_ref, gain_ref, bias_ref, *refs,
):
    outs, scratch = refs[-18:-7], refs[-7:]
    pieces = [refs[0:3], refs[3:8], refs[8:13], refs[13:18]]
    low_ref, z1_ref, r1_ref, saved_ref, z2_ref, r2_ref, sums_ref = outs[:7]
    whole_outs = outs[7:]
    wholes, (sems, out_sems) = scratch[:4], scratch[5:]
    wo_ref, wg_ref, wu_ref, wd_ref = wholes
    tile = pl.program_id(0)
    copies = [
        piece_copies(meta, pieces[at][0].shape[0], pieces[at], wholes[at], sems.at[at])
        for at in range(4)
    ]
    keeps = [
        pltpu.make_async_copy(wholes[at], whole_outs[at], out_sems.at[at]) for at in range(4)
    ]

    @pl.when(tile == 0)
    def _():
        for group in copies:
            for copy in group:
                copy.start()

    def ready(which):
        @pl.when(tile == 0)
        def _():
            for at in which:
                for copy in copies[at]:
                    copy.wait()
                keeps[at].start()

    ready((0,))

    @pl.when(tile < meta[TILES])
    def _():
        z1, r1 = normalize(x_ref[...].astype(F32) + dot(att_ref[...], wo_ref[...]))
        z1_ref[...] = z1.astype(BF16)
        r1_ref[...] = r1
        normed = z1 * gain_ref[...] + bias_ref[...]
        low_ref[...] = normed.astype(BF16)
        scratch[4][...] = normed

    ready((1, 2, 3))

    @pl.when(tile < meta[TILES])
    def _():
        low = low_ref[...]
        total = scratch[4][...]
        inner, chunk = wg_ref.shape[1], SPAN
        chunks = inner // (2 * chunk)

        def products(at):
            columns = slice(at, at + chunk)
            return dot(low, wg_ref[:, columns]), dot(low, wu_ref[:, columns])

        ahead = products(0)
        for at in range(0, inner, chunk):
            columns = slice(at, at + chunk)
            gate, up = ahead
            if at + chunk < inner:
                ahead = products(at + chunk)
            sigmoid = 0.5 * jnp.tanh(0.5 * gate) + 0.5
            silu = gate * sigmoid
            hidden = (silu * up).astype(BF16)
            slope = (up * (sigmoid + silu * (1.0 - sigmoid))).astype(BF16)
            which = at // chunk
            for kind, value in enumerate((hidden, silu.astype(BF16), slope)):
                to = ((which % chunks) * 6 + kind * 2 + which // chunks) * chunk
                saved_ref[:, to : to + chunk] = value
            total = total + dot(hidden, wd_ref[columns, :])
        z2, r2 = normalize(total)
        z2_ref[...] = z2.astype(BF16)
        r2_ref[...] = r2
        half = BLOCK // 2
        inside = lax.broadcasted_iota(jnp.int32, (half, z2.shape[1]), 0)
        for group in range(TILE // half):
            valid = counts[tile * (TILE // half) + group]
            kept = jnp.where(inside < valid, z2[group * half : (group + 1) * half, :], 0.0)
            sums_ref[group : group + 1, :] = jnp.sum(kept, axis=0, keepdims=True)
        sums_ref[TILE // half :, :] = jnp.zeros((8 - TILE // half, z2.shape[1]), F32)

    @pl.when(tile == pl.num_programs(0) - 1)
    def _():
        for keep in keeps:
            keep.wait()


def forward(meta, counts, att, x, pieces, gain, bias, after=()):
    rows, width = x.shape
    inner = pieces[1][0].shape[1]
    wholes = [(width, width), (width, inner), (width, inner), (inner, width)]

    def array(columns, kind):
        return jax.ShapeDtypeStruct((rows, columns), kind)

    grid_spec = pltpu.PrefetchScalarGridSpec(
        num_scalar_prefetch=2,
        grid=(rows // TILE,),
        in_specs=[tiled(width), tiled(width)]
        + [resident(gain.shape), resident(bias.shape)]
        + anywhere(18 + len(after)),
        out_specs=[
            tiled(width), tiled(width), tiled(1), tiled(3 * inner), tiled(width), tiled(1),
            pl.BlockSpec((8, width), lambda i, m, *_: (live(i, m), 0)),
        ]
        + anywhere(4),
        scratch_shapes=[pltpu.VMEM(shape, BF16) for shape in wholes]
        + [
            pltpu.VMEM((TILE, width), F32),
            pltpu.SemaphoreType.DMA((4, 5)),
            pltpu.SemaphoreType.DMA((4,)),
        ],
    )
    return pl.pallas_call(
        forward_kernel,
        grid_spec=grid_spec,
        out_shape=[
            array(width, BF16), array(width, BF16), array(1, F32), array(3 * inner, BF16),
            array(width, BF16), array(1, F32),
            jax.ShapeDtypeStruct((rows // TILE * 8, width), F32),
        ]
        + [jax.ShapeDtypeStruct(shape, BF16) for shape in wholes],
        compiler_params=params(52),
        cost_estimate=cost(42),
        name="forward",
    )(meta, counts, att, x, gain, bias, *[p for group in pieces for p in group], *after)


def norm_two_back(counts, owner, tile, z_ref, r_ref, scaled_ref):
    half = BLOCK // 2
    width = z_ref.shape[1]
    inside = lax.broadcasted_iota(jnp.int32, (half, width), 0)
    grads = []
    for group in range(TILE // half):
        at = tile * (TILE // half) + group
        rows = slice(group * half, (group + 1) * half)
        scaled = scaled_ref[pl.ds(owner[at], 1), :]
        z = z_ref[rows, :].astype(F32)
        plain = jnp.mean(scaled, axis=-1, keepdims=True)
        cross = jnp.mean(scaled * z, axis=-1, keepdims=True)
        grad = r_ref[rows, :] * (scaled - plain - z * cross)
        grads.append(jnp.where(inside < counts[at], grad, 0.0))
    return jnp.concatenate(grads, axis=0)


def ffn_back_kernel(starts, meta, counts, owner, *refs):
    @pl.when(pl.program_id(0) < meta[TILES])
    def _():
        ffn_back_tile(starts, meta, counts, owner, *refs)


def ffn_back_tile(
    starts, meta, counts, owner, low_ref, saved_ref, wd0, wd1, wg0, wg1, wu0, wu1, *refs,
):
    tile = pl.program_id(0)
    span = wd0.shape[0]
    acc_g, acc_u, acc_d, wd_turned, wg_turned, wu_turned = refs[-6:]
    keep_ref, send_ref = refs[-8:-6]
    part_out = refs[-9]
    width = low_ref.shape[1]

    @pl.when(tile == 0)
    def _():
        acc_g[...] = jnp.zeros_like(acc_g)
        acc_u[...] = jnp.zeros_like(acc_u)
        acc_d[...] = jnp.zeros_like(acc_d)
        for half, (wd, wg, wu) in enumerate(((wd0, wg0, wu0), (wd1, wg1, wu1))):
            columns = slice(half * span, (half + 1) * span)
            wd_turned[:, columns] = wd[...].T
            wg_turned[columns, :] = wg[...].T
            wu_turned[columns, :] = wu[...].T

    if starts:
        branch = norm_two_back(counts, owner, tile, *refs[:3]).astype(BF16)
        part_out[:, :width] = branch
    else:
        branch = refs[0][...]
    low_t = low_ref[...].T
    branch_t = branch.T
    hiddens = [
        dot(branch, wd_turned[:, half * span : (half + 1) * span]) for half in range(2)
    ]
    total = None
    for half in range(2):
        columns = slice(half * span, (half + 1) * span)
        hid, silu, slope = (
            saved_ref[:, (kind * 2 + half) * span : (kind * 2 + half + 1) * span] for kind in range(3)
        )
        acc_d[:, columns] += dot(branch_t, hid)
        grad_hidden = hiddens[half]
        grad_gate = (grad_hidden * slope.astype(F32)).astype(BF16)
        grad_up = (grad_hidden * silu.astype(F32)).astype(BF16)
        part = dot(grad_gate, wg_turned[columns, :]) + dot(grad_up, wu_turned[columns, :])
        total = part if total is None else total + part
        acc_g[:, columns] += dot(low_t, grad_gate)
        acc_u[:, columns] += dot(low_t, grad_up)
    part_out[:, part_out.shape[1] - width :] = total.astype(BF16)

    @pl.when(tile == meta[TILES] - 1)
    def _():
        rows, quarter = acc_g.shape[0] // 4, acc_g.shape[0] // 4
        side, row, core = meta[SIDE], meta[ROW], meta[CORE]
        for other_core, out in ((0, keep_ref), (1, send_ref)):
            columns = pl.ds(pl.multiple_of((core ^ other_core) * span, span), span)
            inner = pl.ds(
                pl.multiple_of((core ^ other_core) * (span // 2), span // 2), span // 2
            )
            for other_side in range(2):
                for other_row in range(2):
                    at = (side ^ other_side) * 2 + (row ^ other_row)
                    lines = pl.ds(pl.multiple_of(at * quarter, quarter), quarter)
                    out[other_side, other_row, 0] = acc_g[lines, columns].astype(BF16)
                    out[other_side, other_row, 1] = acc_u[lines, columns].astype(BF16)
                    left = pl.multiple_of(
                        (side ^ other_side) * span + (core ^ other_core) * (span // 2), span // 2
                    )
                    for part in range(2):
                        lines = pl.ds(
                            pl.multiple_of((row ^ other_row) * 2 * quarter + part * quarter, quarter),
                            quarter,
                        )
                        out[
                            other_side, other_row, 2, :, part * (span // 2) : (part + 1) * (span // 2)
                        ] = acc_d[lines, pl.ds(left, span // 2)].astype(BF16)


def ffn_back(meta, counts, owner, chunk, low, saved, wd, wg, wu, given, after=()):
    rows, width = low.shape
    inner, span = wg.shape[1], SPAN
    starts = len(given) == 3
    halves = (chunk, chunk + inner // (2 * span))

    def fixed(shape, index):
        return pl.BlockSpec(shape, lambda i, *_: index, pipeline_mode=pl.Buffered(1))

    if starts:
        given_specs = [tiled(width), tiled(1), resident(given[2].shape)]
    else:
        given_specs = [tiled(width)] + anywhere(len(given) - 1)
    grid_spec = pltpu.PrefetchScalarGridSpec(
        num_scalar_prefetch=3,
        grid=(rows // TILE,),
        in_specs=[tiled(width), tiled(6 * span, chunk)]
        + [fixed((span, width), (at, 0)) for at in halves]
        + [fixed((width, span), (0, at)) for _ in range(2) for at in halves]
        + given_specs
        + anywhere(len(after)),
        out_specs=[tiled(2 * width) if starts else tiled(width, len(given) - 1)]
        + [pl.BlockSpec((2, 2, 3, width // 4, span), lambda i, *_: (0, 0, 0, 0, 0))] * 2,
        scratch_shapes=[pltpu.VMEM((width, 2 * span), F32)] * 3
        + [pltpu.VMEM((width, 2 * span), BF16)]
        + [pltpu.VMEM((2 * span, width), BF16)] * 2,
    )
    piece = jax.ShapeDtypeStruct((2, 2, 3, width // 4, span), BF16)
    return pl.pallas_call(
        functools.partial(ffn_back_kernel, starts),
        grid_spec=grid_spec,
        out_shape=[jax.ShapeDtypeStruct((rows, 2 * width), BF16), piece, piece],
        input_output_aliases={12: 0} if len(given) == 2 else {},
        compiler_params=params(44),
        cost_estimate=cost(23),
        name="ffn_back",
    )(
        meta, counts, owner, low, saved, wd, wd, wg, wg, wu, wu, *given, *after,
    )


def out_pieces(meta, acc, keep_ref, send_ref):
    part = acc.shape[0] // 8
    side, row, core = meta[SIDE], meta[ROW], meta[CORE]
    for other_core, out in ((0, keep_ref), (1, send_ref)):
        for other_side in range(2):
            for other_row in range(2):
                at = ((side ^ other_side) * 2 + (row ^ other_row)) * 2 + (core ^ other_core)
                lines = pl.ds(pl.multiple_of(at * part, part), part)
                out[other_side, other_row, :, : acc.shape[1]] = acc[lines, :].astype(BF16)


@while_live
def norm_one_back_kernel(
    meta, head_ref, tail_ref, z_ref, r_ref, att_ref, gain_ref, wo_ref, later_ref, *refs,
):
    sum_ref, att_grad_ref, gains_out, keep_ref, send_ref, acc, wo_turned = refs[-7:]
    tile = pl.program_id(0)

    @pl.when(tile == 0)
    def _():
        acc[...] = jnp.zeros_like(acc)
        gains_out[...] = later_ref[...]
        wo_turned[...] = wo_ref[...].T

    width = wo_ref.shape[0]
    first = sum(ref[:, at : at + width].astype(F32) for ref in (head_ref, tail_ref) for at in (0, width))
    z = z_ref[...].astype(F32)
    scaled = first * gain_ref[...]
    plain = jnp.mean(scaled, axis=-1, keepdims=True)
    cross = jnp.mean(scaled * z, axis=-1, keepdims=True)
    grad = r_ref[...] * (scaled - plain - z * cross)
    sum_ref[...] = grad
    low = grad.astype(BF16)
    att_grad_ref[...] = dot(low, wo_turned[...]).astype(BF16)
    acc[...] += dot(att_ref[...].T, low)
    gains_out[0:1, :] += jnp.sum(first * z, axis=0, keepdims=True)
    gains_out[1:2, :] += jnp.sum(first, axis=0, keepdims=True)

    @pl.when(tile == meta[TILES] - 1)
    def _():
        out_pieces(meta, acc, keep_ref, send_ref)


def norm_one_back(meta, terms, z, recip, att, gain, wo, later, after=()):
    rows, width = z.shape
    block = (2, 2, width // 8, width)
    piece = jax.ShapeDtypeStruct(block, BF16)
    grid_spec = pltpu.PrefetchScalarGridSpec(
        num_scalar_prefetch=1,
        grid=(rows // TILE,),
        in_specs=[tiled(2 * width), tiled(2 * width), tiled(width)]
        + [tiled(1), tiled(width)]
        + [resident(gain.shape), resident(wo.shape), resident(later.shape)]
        + anywhere(len(after)),
        out_specs=[tiled(width), tiled(width), pl.BlockSpec((8, width), lambda i, *_: (0, 0))]
        + [pl.BlockSpec(block, lambda i, *_: (0, 0, 0, 0))] * 2,
        scratch_shapes=[pltpu.VMEM((width, width), F32), pltpu.VMEM((width, width), BF16)],
    )
    return pl.pallas_call(
        norm_one_back_kernel,
        grid_spec=grid_spec,
        out_shape=[
            jax.ShapeDtypeStruct((rows, width), F32), jax.ShapeDtypeStruct((rows, width), BF16),
            jax.ShapeDtypeStruct((8, width), F32), piece, piece,
        ],
        compiler_params=params(28),
        cost_estimate=cost(12),
        name="norm_one_back",
    )(meta, *terms, z, recip, att, gain, wo, later, *after)


def attend_back_kernel(meta, q_ref, k_ref, v_ref, g_ref, att_ref, lse_ref, cos_ref, sin_ref, *refs):
    out_ref, key_acc, value_acc = refs[-3:]

    def turn_back(grad, table):
        cosine, sine = cos_ref[table, :], sin_ref[table, :]
        return (grad * cosine - swap_halves(grad) * sine).astype(BF16)

    def products(start, size, keys, values, limit, masked):
        rows = pl.ds(start, size)
        queries, grads = split_pair(q_ref[rows, :]), split_pair(g_ref[rows, :])
        log_norm = jnp.concatenate([lse_ref[0, 0:1, rows], lse_ref[0, 1:2, rows]], axis=1)
        if limit is not None:
            column = lax.broadcasted_iota(jnp.int32, log_norm.shape, 1) % size
            log_norm = jnp.where(column < limit, log_norm, -MASKED)
        both = g_ref[rows, :].astype(F32) * att_ref[rows, :].astype(F32)
        head = lax.broadcasted_iota(jnp.int32, (8, 128), 1) // HEAD
        ones = (head == lax.broadcasted_iota(jnp.int32, (8, 128), 0)).astype(F32)
        inner = lax.dot_general(
            ones, both, (((1,), (1,)), ((), ())), precision=lax.Precision.HIGHEST, preferred_element_type=F32
        )
        inner = jnp.concatenate([inner[0:1, :], inner[1:2, :]], axis=1)
        scores = masked(dot(keys, queries, ((1,), (1,))))
        grad_probs = dot(values, grads, ((1,), (1,)))
        return queries, grads, log_norm, inner, scores, grad_probs

    def finish(queries, grads, log_norm, inner, scores, grad_probs, keys_split):
        probs = jnp.exp(scores - log_norm)
        grad_scores = (probs * (grad_probs - inner)).astype(BF16)
        grad_query = (dot(keys_split, stack_heads(grad_scores)) * HEAD**-0.5).T
        return grad_query, dot(grad_scores, queries), dot(probs.astype(BF16), grads)

    @pl.loop(0, 2)
    def _(doc):
        start = pl.multiple_of(meta[OFF0 + doc], BLOCK)
        for blocks in range(1, 7):

            @pl.when(meta[CNT0 + doc] == blocks)
            def _():
                size = blocks * BLOCK
                whole = pl.ds(start, size)
                keys, values = k_ref[whole, :], v_ref[whole, :]
                keys_split = split_turned(keys)
                valid = meta[LEN0 + doc] - (blocks - 1) * BLOCK
                steps = (blocks + 1) // 2

                def ahead_of(step):
                    return products(
                        pl.multiple_of(start + step * TILE, BLOCK), TILE, keys, values,
                        size - step * TILE if size < (step + 1) * TILE else None,
                        lambda scores: mask_keys(scores, blocks - 1, valid),
                    )

                ahead = ahead_of(0)
                for step in range(steps):
                    now = ahead
                    if step + 1 < steps:
                        ahead = ahead_of(step + 1)
                    grad_query, grad_key, grad_value = finish(*now, keys_split)
                    if step > 0:
                        grad_key += key_acc[:size, :]
                        grad_value += value_acc[:size, :]
                    if step + 1 < steps:
                        key_acc[:size, :] = grad_key
                        value_acc[:size, :] = grad_value
                    for sub in range(2):
                        at = pl.multiple_of(start + step * TILE + sub * BLOCK, BLOCK)
                        out_ref[pl.ds(at, BLOCK), 0:128] = turn_back(
                            grad_query[sub * BLOCK : (sub + 1) * BLOCK, :],
                            pl.ds((step * 2 + sub) * BLOCK, BLOCK),
                        )
                out_ref[whole, 128:256] = turn_back(grad_key, pl.ds(0, size))
                out_ref[whole, 256:384] = grad_value.astype(BF16)

    first = pl.multiple_of(meta[OFFQ], BLOCK)
    rows = pl.ds(first, BLOCK)
    keys = k_ref[rows, :]
    grad_query, grad_key, grad_value = finish(
        *products(first, BLOCK, keys, v_ref[rows, :], None, functools.partial(query_mask, meta)),
        split_turned(keys),
    )
    table = pl.ds(cos_ref.shape[0] - BLOCK, BLOCK)
    out_ref[rows, 0:128] = turn_back(grad_query, table)
    out_ref[rows, 128:256] = turn_back(grad_key, table)
    out_ref[rows, 256:384] = grad_value.astype(BF16)
    out_ref[pl.ds(first + BLOCK, BLOCK), :] = jnp.zeros((BLOCK, 384), BF16)


def attend_back(meta, pair, qkv, grad, att, lse, tables, before=(), after=()):
    rows, width = grad.shape
    pairs = width // 128

    def column(part, columns=128):
        return pl.BlockSpec((rows, columns), lambda h, *_: (0, part * pairs + pair))

    grid_spec = pltpu.PrefetchScalarGridSpec(
        num_scalar_prefetch=1,
        grid=(1,),
        in_specs=[
            column(0), column(1), column(2), column(0),
            column(0),
            pl.BlockSpec((1, 8, rows), lambda h, *_: (pair, 0, 0)),
            resident(tables[0].shape), resident(tables[1].shape),
        ]
        + anywhere(len(before) + len(after)),
        out_specs=pl.BlockSpec((rows, 384), lambda h, *_: (0, pair)),
        scratch_shapes=[pltpu.VMEM((6 * BLOCK, 128), F32)] * 2,
    )
    return pl.pallas_call(
        attend_back_kernel,
        grid_spec=grid_spec,
        out_shape=jax.ShapeDtypeStruct((rows, 3 * width), BF16),
        input_output_aliases={9: 0} if before else {},
        compiler_params=params(44),
        cost_estimate=cost(11),
        name="attend_back",
    )(meta, qkv, qkv, qkv, grad, att, lse, *tables, *before, *after)


@while_live
def qkv_grad_kernel(meta, x_ref, *refs):
    keep_ref, send_ref, acc = refs[-3:]
    columns = acc.shape[1]
    pairs = columns // 384
    grad_ref, extra = refs[0], refs[1:3]
    tile = pl.program_id(0)

    @pl.when(tile == 0)
    def _():
        acc[...] = jnp.zeros_like(acc)

    grad = jnp.concatenate(
        [
            grad_ref[:, (pair * 3 + part) * 128 : (pair * 3 + part + 1) * 128]
            for part in range(3)
            for pair in range(pairs)
        ],
        axis=1,
    )
    acc[...] += dot(x_ref[...].T, grad)

    @pl.when(tile == meta[TILES] - 1)
    def _():
        out_pieces(meta, acc, keep_ref, send_ref)
        if keep_ref.shape[3] > columns:
            keep_ref[:, :, :, columns:] = extra[0][...]
            send_ref[:, :, :, columns:] = extra[1][...]


def qkv_grad(meta, x, grad, columns, at, extra=(), after=()):
    rows, width = x.shape
    block = (2, 2, width // 8, columns + sum(part.shape[3] for part in extra[:1]))
    piece = jax.ShapeDtypeStruct(block, BF16)
    grid_spec = pltpu.PrefetchScalarGridSpec(
        num_scalar_prefetch=1,
        grid=(rows // TILE,),
        in_specs=[tiled(width)]
        + [tiled(columns, at)]
        + [resident(part.shape) for part in extra]
        + anywhere(len(after)),
        out_specs=[pl.BlockSpec(block, lambda i, *_: (0, 0, 0, 0))] * 2,
        scratch_shapes=[pltpu.VMEM((width, columns), F32)],
    )
    return pl.pallas_call(
        qkv_grad_kernel,
        grid_spec=grid_spec,
        out_shape=[piece, piece],
        compiler_params=params(44),
        cost_estimate=cost(9),
        name="qkv_grad",
    )(meta, x, grad, *extra, *after)


def token_grad_kernel(which, meta, *refs):
    sums, grads, weight = refs[0:2], refs[2:4], refs[4]
    step = pl.program_id(0)

    def value():
        total = jnp.concatenate([part[...] for part in sums], axis=0)
        return total + dot(jnp.concatenate([part[...] for part in grads], axis=0), weight[...])

    if which == 0:
        docs_ref = refs[-1]
        length = meta[LEN0] - step * TILE
        store = lambda value: docs_ref.__setitem__(0, value)
    else:
        docs_ref, queries_ref = refs[-2:]
        length = jnp.where(step < 3, meta[LEN1] - step * TILE, TILE)
        store = lambda value: docs_ref.__setitem__(slice(None), value.astype(BF16))

    @pl.when((step < 3) & (length > 0))
    def _():
        total = value()
        inside = lax.broadcasted_iota(jnp.int32, total.shape, 0)
        store(jnp.where(inside < length, total, 0.0))

    @pl.when((step < 3) & (length <= 0))
    def _():
        store(jnp.zeros((TILE, docs_ref.shape[-1]), F32))

    if which == 1:

        @pl.when(step == 3)
        def _():
            total = value()[:BLOCK, :]
            inside = lax.broadcasted_iota(jnp.int32, (BLOCK // 2, total.shape[1]), 0)
            for query in range(2):
                half = total[query * (BLOCK // 2) : (query + 1) * (BLOCK // 2), :]
                queries_ref[query] = jnp.where(inside < meta[QLEN0 + query], half, 0.0)


def token_grad(which, meta, sums, grad, weight, after=()):
    rows, width = sums.shape

    def block_of(step, meta, second):
        last = meta[CNT0 + which] - 1
        in_doc = jnp.minimum(jnp.minimum(step, 2) * 2 + second, last)
        return jnp.where(step < 3, meta[OFF0 + which] // BLOCK + in_doc, meta[OFFQ] // BLOCK)

    def halves(columns):
        return [
            pl.BlockSpec((BLOCK, columns), lambda i, meta, s=s: (block_of(i, meta, s), 0)) for s in range(2)
        ]

    if which == 0:
        out_specs = [pl.BlockSpec((1, TILE, width), lambda i, meta: (1 - meta[SLOT], i, 0))]
        out_shape = [jax.ShapeDtypeStruct((2, 6 * BLOCK, width), F32)]
    else:
        out_specs = [
            pl.BlockSpec((TILE, width), lambda i, meta: (jnp.minimum(i, 2), 0)),
            pl.BlockSpec((2, BLOCK // 2, width), lambda i, meta: (0, 0, 0)),
        ]
        out_shape = [
            jax.ShapeDtypeStruct((6 * BLOCK, width), BF16),
            jax.ShapeDtypeStruct((2, BLOCK // 2, width), F32),
        ]
    grid_spec = pltpu.PrefetchScalarGridSpec(
        num_scalar_prefetch=1,
        grid=(3 + which,),
        in_specs=halves(width) + halves(grad.shape[1]) + [resident(weight.shape)]
        + anywhere(len(after)),
        out_specs=out_specs,
    )
    return pl.pallas_call(
        functools.partial(token_grad_kernel, which),
        grid_spec=grid_spec,
        out_shape=out_shape,
        compiler_params=params(44),
        cost_estimate=cost(9),
        name="token_grad",
    )(meta, sums, sums, grad, grad, weight, *after)


def place_moved_kernel(meta, own_ref, other_ref, *refs):
    docs_ref = refs[-1]

    @pl.when(meta[STAY] == 1)
    def _():
        docs_ref[0] = own_ref[...].astype(F32)

    @pl.when(meta[STAY] == 0)
    def _():
        docs_ref[0] = other_ref[...].astype(F32)


def place_moved(meta, docs, own, other, after=()):
    width = docs.shape[2]
    grid_spec = pltpu.PrefetchScalarGridSpec(
        num_scalar_prefetch=1,
        grid=(3,),
        in_specs=[pl.BlockSpec((TILE, width), lambda i, m: (i, 0))] * 2 + anywhere(1 + len(after)),
        out_specs=pl.BlockSpec((1, TILE, width), lambda i, m: (m[SLOT], i, 0)),
    )
    return pl.pallas_call(
        place_moved_kernel,
        grid_spec=grid_spec,
        out_shape=jax.ShapeDtypeStruct(docs.shape, F32),
        input_output_aliases={3: 0},
        compiler_params=params(16),
        cost_estimate=cost(4),
        name="place_moved",
    )(meta, own, other, docs, *after)


def plan_kernel(place, own_ref, across_ref, queries_ref, meta, table_block, counts, owner):
    core = place[0]
    half = BLOCK // 2
    number = [
        jnp.where(core == 0, own_ref[at], across_ref[at]) if at < 2
        else jnp.where(core == 0, across_ref[at - 2], own_ref[at - 2])
        for at in range(4)
    ]
    blocks = [(count + BLOCK - 1) // BLOCK for count in number]
    work = [count * (10 + count) for count in blocks]
    total = work[0] + work[1] + work[2] + work[3]
    loads = [jnp.maximum(work[0] + work[at], total - work[0] - work[at]) for at in (1, 2, 3)]
    plan = jnp.where(
        (loads[0] <= loads[1]) & (loads[0] <= loads[2]), 0, jnp.where(loads[1] <= loads[2], 1, 2)
    )
    stay = jnp.where(plan == 0, 1, 0)
    far_slot = jnp.where(plan == 1, 0, 1)
    slot = jnp.where(core == 0, 1, far_slot)
    slot_there = jnp.where(core == 0, far_slot, 1)
    first = jnp.where(slot == 1, own_ref[0], own_ref[1])
    here = jnp.where(slot == 1, own_ref[1], own_ref[0])
    there = jnp.where(slot_there == 1, across_ref[1], across_ref[0])
    second = jnp.where(stay == 1, here, there)
    first_blocks, second_blocks = (first + BLOCK - 1) // BLOCK, (second + BLOCK - 1) // BLOCK
    end = first_blocks + second_blocks
    device = place[3]
    other = jnp.where(core == 0, device + 1, device - 1)
    values = [
        0, first_blocks * BLOCK, end * BLOCK, first, second, queries_ref[0], queries_ref[1],
        first_blocks, second_blocks, (end + 2) // 2, core, place[1], place[2], slot, stay,
        2 * device, 2 * device + 1, 2 * device + 1 - slot,
        jnp.where(stay == 1, 2 * device + slot, 2 * other + slot_there),
    ]
    for at, value in enumerate(values):
        meta[at] = jnp.int32(value)
    for at in range(len(values), meta.shape[0]):
        meta[at] = 0
    for at in range(table_block.shape[0]):
        table_block[at] = jnp.where(
            at < first_blocks, at, jnp.where(at < end, at - first_blocks, 6)
        )
    for at in range(counts.shape[0]):
        in_first, in_second = at < 2 * first_blocks, at < 2 * end
        query = at - 2 * end
        count = jnp.where(
            in_first,
            first - at * half,
            jnp.where(
                in_second,
                second - (at - 2 * first_blocks) * half,
                jnp.where(query == 0, queries_ref[0], jnp.where(query == 1, queries_ref[1], 0)),
            ),
        )
        counts[at] = jnp.clip(count, 0, half)
        owner[at] = jnp.where(in_first, 2, jnp.where(in_second, 3, jnp.clip(query, 0, 1)))


def layout(place, doc_counts, across, query_counts, rows):
    smem = pl.BlockSpec(memory_space=pltpu.SMEM)
    half_blocks = rows // (BLOCK // 2)
    return pl.pallas_call(
        plan_kernel,
        in_specs=[smem] * 4,
        out_specs=[smem] * 4,
        out_shape=[
            jax.ShapeDtypeStruct((length,), jnp.int32)
            for length in (24, rows // BLOCK, half_blocks, half_blocks)
        ],
        cost_estimate=cost(1),
        name="plan",
    )(place, doc_counts, across, query_counts)


def pack_kernel(meta, docs, received, queries, out, sems):
    stay, slot = meta[STAY], meta[SLOT]

    def copies():
        for block in range(docs.shape[1] // BLOCK):
            lines = pl.ds(block * BLOCK, BLOCK)
            to = out.at[pl.ds(pl.multiple_of(meta[OFF1] + block * BLOCK, BLOCK), BLOCK)]
            second = block < meta[CNT1]
            yield block < meta[CNT0], docs.at[1 - slot, lines], out.at[lines], sems.at[0, block]
            yield second & (stay == 1), docs.at[slot, lines], to, sems.at[1, block]
            yield second & (stay == 0), received.at[lines], to, sems.at[2, block]
        end = pl.multiple_of(meta[OFFQ], BLOCK)
        yield None, queries, out.at[pl.ds(end, BLOCK)], sems.at[3, 0]

    out[pl.ds(pl.multiple_of(meta[OFFQ] + BLOCK, BLOCK), BLOCK), :] = jnp.zeros((BLOCK, out.shape[1]), out.dtype)
    for step in ("start", "wait"):
        for needed, source, to, sem in copies():
            copy = pltpu.make_async_copy(source, to, sem)
            if needed is None:
                getattr(copy, step)()
            else:
                pl.when(needed)(getattr(copy, step))


def pack_rows(meta, docs, received, queries, rows):
    width = docs.shape[2]
    return pl.pallas_call(
        pack_kernel,
        in_specs=[pl.BlockSpec(memory_space=pltpu.SMEM)] + anywhere(3),
        out_specs=pl.BlockSpec(memory_space=pltpu.VMEM),
        out_shape=jax.ShapeDtypeStruct((rows, width), docs.dtype),
        scratch_shapes=[pltpu.SemaphoreType.DMA((4, docs.shape[1] // BLOCK))],
        compiler_params=pltpu.CompilerParams(vmem_limit_bytes=16 * 1024 * 1024),
        cost_estimate=cost(2),
        name="pack",
    )(meta, docs, received, queries.reshape(BLOCK, width))


def by_row(shape, values):
    row = lax.broadcasted_iota(jnp.int32, shape, 0) % 4
    first, second, third, fourth = (jnp.full(shape, value) for value in values)
    return jnp.where(row == 0, first, jnp.where(row == 1, second, jnp.where(row == 2, third, fourth)))


def lengths_of(meta):
    lengths = by_row((8, 128), [meta[QLEN0], meta[QLEN1], meta[LEN0], meta[LEN1]])
    return lengths[:, 0:1].astype(F32)


def unit_kernel(meta, owner, index, weights, sums_ref, gain_ref, bias_ref, message_ref, pooled_ref, sums_out, recip_ref):
    rows, width = sums_ref.shape
    shape = (8, 128)
    lane = lax.broadcasted_iota(jnp.int32, shape, 1)
    weight = by_row(shape, [weights[0], weights[1], jnp.float32(0.0), jnp.float32(0.0)])
    high = jnp.floor(weight * 16.0)
    rest = (weight * 16.0 - high) * 256.0
    middle = jnp.floor(rest)
    lowest = jnp.floor((rest - middle) * 256.0)
    number = by_row(shape, [meta[IDS + at] for at in range(4)]).astype(F32)
    partner = by_row(shape, [index[0], index[1], jnp.int32(0), jnp.int32(0)]).astype(F32)
    extra = jnp.zeros(shape, F32)
    for at, value in enumerate((number, partner, high, middle, lowest)):
        extra = jnp.where(lane == at, value, extra)
    per_tile = TILE // (BLOCK // 2)
    line = lax.broadcasted_iota(jnp.int32, (8, rows), 0) % 4
    column = lax.broadcasted_iota(jnp.int32, (8, rows), 1)
    pick = jnp.zeros((8, rows), F32)
    for group in range(rows // 8 * per_tile):
        at = group // per_tile * 8 + group % per_tile
        here = (column == at) & (line == owner[group]) & (group // per_tile < meta[TILES])
        pick = jnp.where(here, 1.0, pick)
    lengths = lengths_of(meta)
    inside = lax.broadcasted_iota(jnp.int32, (rows, width), 0) < 8 * meta[TILES]
    sums = lax.dot_general(
        pick, jnp.where(inside, sums_ref[...], 0.0), (((1,), (0,)), ((), ())),
        precision=lax.Precision.HIGHEST, preferred_element_type=F32,
    )
    pooled = sums / lengths * gain_ref[...] + bias_ref[...]
    recip = lax.rsqrt(jnp.sum(pooled * pooled, axis=1, keepdims=True) + EPS_UNIT)
    unit = (pooled * recip).astype(BF16)
    half = width // 2
    upper = lax.broadcasted_iota(jnp.int32, (8, half), 0) < 4
    message_ref[:, :half] = jnp.where(upper, unit[:, :half].astype(F32), unit[:, half:].astype(F32)).astype(BF16)
    message_ref[:, half:] = extra.astype(BF16)
    pooled_ref[...] = pooled
    sums_out[...] = sums
    recip_ref[...] = jnp.broadcast_to(recip, recip_ref.shape)


def units(meta, owner, index, weights, sums, gain, bias):
    vmem = pl.BlockSpec(memory_space=pltpu.VMEM)
    width = sums.shape[1]
    return pl.pallas_call(
        unit_kernel,
        in_specs=[pl.BlockSpec(memory_space=pltpu.SMEM)] * 4 + [vmem] * 3,
        out_specs=[vmem] * 4,
        out_shape=[
            jax.ShapeDtypeStruct((8, width // 2 + 128), BF16),
            jax.ShapeDtypeStruct((8, width), F32),
            jax.ShapeDtypeStruct((8, width), F32),
            jax.ShapeDtypeStruct((8, 128), F32),
        ],
        compiler_params=pltpu.CompilerParams(vmem_limit_bytes=16 * 1024 * 1024),
        name="unit",
    )(meta, owner, index, weights, sums, gain, bias)


def loss_kernel(meta, softness, gain_ref, pooled_ref, sums_ref, recip_ref, *refs):
    loss_ref, scaled_ref, later_ref = refs[-3:]
    message = jnp.concatenate([ref[...] for ref in refs[:-3]], axis=0)
    rows, half = message.shape[0], message.shape[1] - 128
    pairs = rows // 4
    soft = softness[0]
    low = message[:, :half]
    extra = message[:, half:].astype(F32)
    row = lax.broadcasted_iota(jnp.int32, (rows, pairs), 0) % 8
    index = (extra[:, 0:1] + 0.5).astype(jnp.int32)
    found = lax.broadcasted_iota(jnp.int32, (rows, pairs), 1) == index
    of_query, of_doc = found & (row % 4 < 2), found & (row % 4 >= 2)

    def gathered(chosen):
        halves = [
            dot((chosen & (row // 4 == which)).astype(F32).astype(BF16), low, ((0,), (0,))) for which in range(2)
        ]
        return jnp.concatenate(halves, axis=1).astype(BF16)

    units_q, units_d = gathered(of_query), gathered(of_doc)
    exact = functools.partial(
        lax.dot_general, precision=lax.Precision.HIGHEST, preferred_element_type=F32
    )
    plain, turned, over_rows = (((1,), (0,)), ((), ())), (((1,), (1,)), ((), ())), (((0,), (0,)), ((), ()))
    extra = exact((of_query & (row < 4)).astype(F32), extra, over_rows)
    weight = extra[:, 2:3] / 16.0 + extra[:, 3:4] / 4096.0 + extra[:, 4:5] / 1048576.0
    similarity = dot(units_q, units_d, ((1,), (1,))) / soft
    columns = lax.broadcasted_iota(jnp.int32, similarity.shape, 1)
    target = (columns == (extra[:, 1:2] + 0.5).astype(jnp.int32)).astype(F32)
    highest = jnp.max(similarity, axis=1, keepdims=True)
    log_norm = highest + jnp.log(jnp.sum(jnp.exp(similarity - highest), axis=1, keepdims=True))
    picked = jnp.sum(target * similarity, axis=1, keepdims=True)
    loss = jnp.sum(weight * (log_norm - picked), axis=0, keepdims=True) / pairs
    loss_ref[...] = jnp.broadcast_to(loss, loss_ref.shape)
    grad = weight * (jnp.exp(similarity - log_norm) - target) / pairs
    line = lax.broadcasted_iota(jnp.int32, (8, pairs), 0)
    column = lax.broadcasted_iota(jnp.int32, (8, pairs), 1)
    my_queries = (column == jnp.where(line == 0, meta[IDS], meta[IDS + 1])) & (line < 2)
    my_docs = (column == jnp.where(line == 2, meta[IDS + 2], meta[IDS + 3])) & (line >= 2) & (line < 4)
    query_rows = exact(my_queries.astype(F32), grad, plain)
    doc_rows = exact(my_docs.astype(F32), grad, turned)
    grad_unit = (
        exact(query_rows, units_d.astype(F32), plain) + exact(doc_rows, units_q.astype(F32), plain)
    ) / soft
    pooled, recip, lengths = pooled_ref[...], recip_ref[:, 0:1], lengths_of(meta)
    crossed = jnp.sum(grad_unit * pooled, axis=1, keepdims=True)
    grad_rows = (recip * grad_unit - pooled * (recip * recip * recip) * crossed) / lengths
    first_half = lax.broadcasted_iota(jnp.int32, grad_rows.shape, 0)
    grad_rows = jnp.where(first_half < 4, grad_rows, 0.0)
    scaled_ref[...] = grad_rows * gain_ref[...]
    gain = jnp.sum(grad_rows * sums_ref[...], axis=0, keepdims=True)
    bias = jnp.sum(grad_rows * lengths, axis=0, keepdims=True)
    later_ref[...] = jnp.where(first_half == 2, gain, jnp.where(first_half == 3, bias, 0.0))


def loss_and_grads(meta, softness, gain, pooled, sums, recip, messages):
    width = pooled.shape[1]
    vmem = pl.BlockSpec(memory_space=pltpu.VMEM)
    return pl.pallas_call(
        loss_kernel,
        in_specs=[pl.BlockSpec(memory_space=pltpu.SMEM)] * 2 + [vmem] * (4 + len(messages)),
        out_specs=[vmem, vmem, vmem],
        out_shape=[
            jax.ShapeDtypeStruct((8, 128), F32),
            jax.ShapeDtypeStruct((8, width), F32),
            jax.ShapeDtypeStruct((8, width), F32),
        ],
        compiler_params=pltpu.CompilerParams(vmem_limit_bytes=24 * 1024 * 1024),
        name="loss",
    )(meta, softness, gain, pooled, sums, recip, *messages)


def wide_unfold_kernel(piece, *refs):
    gate_ref, up_ref, down_ref = refs[-3:]
    gate_ref[...] = piece[0, 0].astype(F32)
    up_ref[...] = piece[0, 1].astype(F32)
    span = piece.shape[3] // 2
    block = jnp.concatenate([piece[0, 2, :, :span], piece[0, 2, :, span:]], axis=0)
    down_ref[...] = block.astype(F32).T


def wide_unfold(chunk, pieces, before, width, inner, after=()):
    quarter, span = pieces.shape[2:]
    chunks = inner // (2 * span)
    place = pl.BlockSpec((quarter, span), lambda i: (i // 2, (i % 2) * chunks + chunk))
    return pl.pallas_call(
        wide_unfold_kernel,
        grid=(4,),
        in_specs=[pl.BlockSpec((1, *pieces.shape[1:]), lambda i: (i, 0, 0, 0))]
        + anywhere(len(before) + len(after)),
        out_specs=[
            place, place,
            pl.BlockSpec((span // 2, 2 * quarter), lambda i: (2 * chunk + i % 2, i // 2)),
        ],
        out_shape=[
            jax.ShapeDtypeStruct((width // 2, inner), F32),
            jax.ShapeDtypeStruct((width // 2, inner), F32),
            jax.ShapeDtypeStruct((inner // 2, width), F32),
        ],
        input_output_aliases={1 + at: at for at in range(len(before))},
        compiler_params=params(16),
        cost_estimate=cost(3),
        name="wide_unfold",
    )(pieces, *before, *after)


def wide_unfold_parts_kernel(meta, p00, p01, p10, p11, *refs):
    gate_ref, up_ref, down_ref = refs[-3:]
    for other_core in range(2):
        for other_row in range(2):
            piece = ((p00, p01), (p10, p11))[other_core][other_row]

            @pl.when((pl.program_id(0) == other_core) & (pl.program_id(1) == other_row))
            def _():
                gate_ref[...] = piece[0].astype(F32)
                up_ref[...] = piece[1].astype(F32)
                span = piece.shape[2] // 2
                block = jnp.concatenate([piece[2, :, :span], piece[2, :, span:]], axis=0)
                down_ref[...] = block.astype(F32).T


def wide_unfold_parts(meta, chunk, pieces, before, width, inner, after=()):
    quarter, span = pieces[0].shape[1:]
    chunks = inner // (2 * span)
    aliased = [pl.BlockSpec(memory_space=pl.ANY)] * len(before)
    grid_spec = pltpu.PrefetchScalarGridSpec(
        num_scalar_prefetch=1,
        grid=(2, 2),
        in_specs=[resident(p.shape) for p in pieces] + aliased + anywhere(len(after)),
        out_specs=[
            pl.BlockSpec(
                (quarter, span), lambda c, r, m: (m[ROW] ^ r, (m[CORE] ^ c) * chunks + chunk)
            )
            for _ in range(2)
        ]
        + [
            pl.BlockSpec(
                (span // 2, 2 * quarter), lambda c, r, m: (2 * chunk + (m[CORE] ^ c), m[ROW] ^ r)
            )
        ],
    )
    return pl.pallas_call(
        wide_unfold_parts_kernel,
        grid_spec=grid_spec,
        out_shape=[
            jax.ShapeDtypeStruct((width // 2, inner), F32),
            jax.ShapeDtypeStruct((width // 2, inner), F32),
            jax.ShapeDtypeStruct((inner // 2, width), F32),
        ],
        input_output_aliases={5 + at: at for at in range(len(before))},
        compiler_params=params(16),
        cost_estimate=cost(3),
        name="wide_unfold_parts",
    )(meta, *pieces, *before, *after)


AXES = ("fsdp", "blk")


class Links:
    def __init__(self, sides, blk):
        self.sides, self.blk, self.outer = sides, blk, blk // 4

    def swap(self, value, side=0, mask=0):
        pairs = [
            (f * self.blk + b, (f ^ side) * self.blk + (b ^ mask))
            for f in range(self.sides)
            for b in range(self.blk)
        ]
        return lax.ppermute(value, AXES, pairs)

    def core(self, value):
        return self.swap(value, mask=1)

    def row(self, value):
        return self.swap(value, mask=2)

    def side(self, value):
        return self.swap(value, side=1)

    def shift(self, value, by):
        pairs = [
            (f * self.blk + b, f * self.blk + (b + 4 * by) % self.blk)
            for f in range(self.sides)
            for b in range(self.blk)
        ]
        return lax.ppermute(value, AXES, pairs)

    def step(self, value, moves):
        pairs = [
            (f * self.blk + 4 * start + b, f * self.blk + 4 * end + b)
            for f in range(self.sides)
            for start, end in moves
            for b in range(4)
        ]
        return lax.ppermute(value, AXES, pairs)

    def outer_masks(self):
        mask = 4
        while mask < self.blk:
            yield mask
            mask *= 2

    def gather(self, value):
        both = jnp.concatenate([value, self.core(value)], axis=0)
        plane = jnp.concatenate(
            [both, self.swap(both, 1, 0), self.swap(both, 0, 2), self.swap(both, 1, 2)], axis=0
        )
        return [plane] + [self.shift(plane, by) for by in range(1, self.outer)]

    def stages(self, keep, send, row_first, by_swaps=False):
        add = lambda *terms: sum(term.astype(F32) for term in terms).astype(BF16)
        now = yield
        now = yield (send := tie(send, now))
        received = tie(self.core(send), now)
        if row_first:
            now = yield (away := add(keep[:, 1], received[:, 1]))
            across = tie(self.row(away), now)
            now = yield (away := add(keep[1, 0], received[1, 0], across[1]))
            last = self.side(away)
        else:
            now = yield (away := add(keep[1], received[1]))
            across = tie(self.side(away), now)
            now = yield (away := add(keep[0, 1], received[0, 1], across[1]))
            last = self.row(away)
        mine = add(keep[0, 0], received[0, 0], across[0], tie(last, now))
        if self.outer == 4:
            outer = lax.axis_index("blk") // 4
            now = yield mine
            mine = add(mine, tie(self.step(mine, ((0, 1), (3, 2))), now))
            now = yield mine
            mine = add(mine, tie(self.step(mine, ((1, 2), (2, 1))), now))
            now = yield mine
            result = tie(self.step(mine, ((1, 0), (2, 3))), now)
            mine = jnp.where((outer == 1) | (outer == 2), mine, result)
        else:
            for mask in self.outer_masks():
                now = yield mine
                mine = add(mine, tie(self.swap(mine, mask=mask), now))
        if by_swaps:
            now = yield mine
            other = tie(self.row(mine), now)
            yield other
            return mine, other, self.core(mine), self.core(other)
        groups = [[at + part for part in range(4)] for at in range(0, self.blk, 4)]
        flat = mine.reshape(-1, mine.shape[-1])
        gathered = lax.all_gather(flat, "blk", axis_index_groups=groups, axis=0, tiled=True)
        yield mine
        return gathered

    def stages_small(self, value):
        now = yield
        for side, mask in [(0, 1), (1, 0), (0, 2)] + [(0, mask) for mask in self.outer_masks()]:
            value = tie(value, now)
            now = yield value
            value = value + self.swap(value, side, mask)
        return value


def tie(value, now):
    return lax.optimization_barrier((value, now))[0]


class Flow:
    def __init__(self):
        self.sums, self.done = {}, {}

    def begin(self, name, stages):
        next(stages)
        self.sums[name] = stages

    def forward(self, now, *names):
        sent = []
        for name in names:
            if name in self.done:
                continue
            try:
                sent.append(self.sums[name].send(now))
            except StopIteration as end:
                self.done[name] = end.value
                if name == "s":
                    sent.append(end.value)
        return tuple(sent)

    def result(self, now, name):
        while name not in self.done:
            self.forward(now, name)
        return self.done[name]


def part_of(share, parts, at):
    size = share.shape[0] // parts
    return lax.dynamic_slice_in_dim(share, at * size, size, 0)


def body(
    question_activations,
    passage_activations,
    question_unpadded_counts,
    passage_unpadded_counts,
    correct_passage_index,
    query_weights,
    softness_factor,
    combined_projection_matrix,
    mixing_result_matrix,
    gating_matrix,
    widening_matrix,
    narrowing_matrix,
    initial_layernorm_scale,
    initial_layernorm_shift,
    later_layernorm_scale,
    later_layernorm_shift,
):
    doc_len, width = passage_activations.shape[1:]
    query_len = question_activations.shape[1]
    inner = gating_matrix.shape[1]
    assert passage_activations.shape[0] == 2 and doc_len == 6 * BLOCK and 2 * query_len == BLOCK
    links = Links(lax.axis_size("fsdp"), lax.axis_size("blk"))
    side, blk = lax.axis_index("fsdp"), lax.axis_index("blk")
    core, row = blk % 2, (blk // 2) % 2

    part_qkv = part_of(combined_projection_matrix, 2, core)
    got_qkv = links.side(part_qkv)
    quarter = row * 2 + core
    part_out = tie(part_of(mixing_result_matrix, 2, core), got_qkv)
    part_gate = tie(part_of(gating_matrix, 4, quarter), got_qkv)
    got_out, got_gate = links.side(part_out), links.side(part_gate)
    rows = -(-(2 * doc_len + BLOCK) // TILE) * TILE
    place = jnp.stack([core, side, row, side * links.blk + blk]).astype(jnp.int32)
    per_chip = tie(passage_unpadded_counts.astype(jnp.int32), part_qkv)
    query_counts = question_unpadded_counts.astype(jnp.int32)
    meta, table_block, counts, owner = layout(place, per_chip, links.core(per_chip), query_counts, rows)
    sent_doc = lax.dynamic_index_in_dim(passage_activations, meta[SLOT], 0, keepdims=False)
    tables = tuple(jnp.asarray(table) for table in rotary_tables(doc_len, query_len))
    x = pack_rows(meta, passage_activations, links.core(sent_doc), question_activations, rows)

    got_qkv = tie(got_qkv, x)
    pieces_qkv = (combined_projection_matrix, got_qkv, links.core(got_qkv))
    qkv, wqkv = project(meta, table_block, x, pieces_qkv, tables, (part_out, part_gate))
    got_out, got_gate = tie((got_out, got_gate), qkv)
    own_vectors = tie(
        (initial_layernorm_scale, initial_layernorm_shift, later_layernorm_scale, later_layernorm_shift),
        qkv,
    )
    vectors = jnp.stack(own_vectors)
    others = links.side(vectors)
    vectors = jnp.concatenate(
        [jnp.where(side == 0, vectors, others), jnp.where(side == 0, others, vectors)], axis=1
    ).astype(F32)
    gain_one, bias_one, gain_two, bias_two = (vectors[at : at + 1] for at in range(4))
    part_up = tie(part_of(widening_matrix, 4, quarter), qkv)
    far_out, along_gate, got_up = links.core(got_out), links.row(got_gate), links.side(part_up)
    heads = attend(meta, qkv, 0, 2, (), (got_out, got_gate, part_up))
    along_gate, got_up = tie((along_gate, got_up), heads[1])
    part_down = tie(part_of(narrowing_matrix, 4, quarter), heads[1])
    far_gate = links.core(got_gate), links.core(along_gate)
    along_up, got_down = links.row(got_up), links.side(part_down)
    heads = attend(meta, qkv, 1, 2, heads, (far_out, along_gate, got_up, part_down))
    along_up, got_down = tie((along_up, got_down), heads[1])
    far_up = links.core(got_up), links.core(along_up)
    along_down = links.row(got_down)
    att, lse = attend(
        meta, qkv, 2, 2, heads, (*far_gate, along_up, got_down, vectors)
    )
    along_down = tie(along_down, lse)
    far_down = links.core(got_down), links.core(along_down)
    weights = [
        (mixing_result_matrix, got_out, far_out),
        (gating_matrix, got_gate, along_gate, *far_gate),
        (widening_matrix, got_up, along_up, *far_up),
        (narrowing_matrix, got_down, along_down, *far_down),
    ]
    low, z1, r1, saved, z2, r2, sums, wo, wg, wu, wd = forward(
        meta, counts, att, x, weights, gain_one, bias_one
    )

    message, pooled, z_sums, recip = units(
        meta, owner, correct_passage_index.astype(jnp.int32), query_weights, sums, gain_two, bias_two
    )
    loss, scaled, later = loss_and_grads(
        meta, softness_factor, gain_two, pooled, z_sums, recip, links.gather(message)
    )
    flow = Flow()

    def wide(chunk, given, after):
        out, keep, send = ffn_back(
            meta, counts, owner, chunk, low, saved, wd, wg, wu, given, after
        )
        flow.begin("w%d" % chunk, links.stages(keep, send, chunk == 2, chunk == 2))
        return out, keep

    def score(pair, before, after):
        return attend_back(meta, pair, qkv, grad_att, att, lse, tables, before, after)

    def narrow(group, columns, at, extra, after):
        keep, send = qkv_grad(meta, x, grads, columns, at, extra, after)
        flow.begin("q%d" % group, links.stages(keep, send, group == 0))
        return keep

    head, now = wide(0, (z2, r2, scaled), ())
    tail, now = wide(1, (head,), flow.forward(now, "w0"))
    tail, now = wide(2, (head, tail), flow.forward(now, "w0", "w1"))
    sum_one, grad_att, now, *mixing = norm_one_back(
        meta, (head, tail), z1, r1, att, gain_one, wo, later, flow.forward(now, "w0", "w1", "w2")
    )
    flow.begin("s", links.stages_small(now))
    grads = score(0, (), flow.forward(now, "w0", "w2"))
    grads = score(1, (grads,), flow.forward(grads, "w0"))
    grads = score(2, (grads,), flow.forward(grads, "w0", "w1"))
    grads = score(3, (grads,), flow.forward(grads, "w0", "w2"))
    now = narrow(0, 1536, 0, mixing, flow.forward(grads, "w1"))
    grads = score(4, (grads,), flow.forward(now, "w1", "w2", "q0"))
    now = grads = score(5, (grads,), flow.forward(grads, "w0", "w1", "w2", "q0"))
    unfold = lambda chunk, before, after: wide_unfold(
        chunk, flow.result(now, "w%d" % chunk).reshape(4, 3, width // 4, -1), before, width, inner, after
    )
    grad_wide = unfold(0, (), ())
    now = narrow(1, 768, 2, (), (*flow.forward(now, "w1", "w2"), grad_wide[0]))
    (grad_docs,) = token_grad(
        0, meta, sum_one, grads, wqkv, flow.forward(now, "w2", "q0", "q1", "s")
    )
    moved, grad_queries = token_grad(
        1, meta, sum_one, grads, wqkv, (grad_docs, *flow.forward(grad_docs, "q0", "q1", "s"))
    )
    other_moved = links.core(moved)
    grad_wide = unfold(1, grad_wide, flow.forward(moved, "w1", "w2", "q0", "q1", "s"))
    now = grad_wide[0]
    grad_docs = place_moved(
        meta, grad_docs, moved, other_moved, (now, *flow.forward(now, "w2", "q0", "q1", "s"))
    )
    after = flow.forward(grad_docs, "q0", "q1", "s")
    grad_wide = wide_unfold_parts(
        meta, 2, flow.result(grad_docs, "w2"), grad_wide, width, inner, (grad_docs, *after)
    )
    while len(flow.done) < 6:
        flow.forward(moved, "q0", "q1", "s")
    first_part, second_part = flow.done["q0"], flow.done["q1"]
    joint = first_part.shape[1] - width
    grad_qkv = jnp.concatenate(
        [
            part.astype(F32)
            for parts in zip(jnp.split(first_part[:, :joint], 3, axis=1), jnp.split(second_part, 3, axis=1))
            for part in parts
        ],
        axis=1,
    )
    grad_out = first_part[:, joint:].astype(F32)
    small = lax.dynamic_slice_in_dim(flow.done["s"], side * (width // 2), width // 2, 1)
    return (
        loss[0, :1],
        grad_queries,
        grad_docs,
        grad_qkv,
        grad_out,
        grad_wide[0],
        grad_wide[1],
        grad_wide[2],
        small[0],
        small[1],
        small[2],
        small[3],
    )


def solution(mesh):
    placed = (
        P(("fsdp", "blk"), None, None),
        P(("fsdp", "blk"), None, None),
        P(("fsdp", "blk")),
        P(("fsdp", "blk")),
        P(("fsdp", "blk")),
        P(("fsdp", "blk")),
        P(),
        P("fsdp", None),
        P("fsdp", None),
        P("fsdp", None),
        P("fsdp", None),
        P("fsdp", None),
        P("fsdp"),
        P("fsdp"),
        P("fsdp"),
        P("fsdp"),
    )
    return jax.shard_map(
        body,
        mesh=mesh,
        in_specs=placed,
        out_specs=(
            P(),
            P(("fsdp", "blk"), None, None),
            P(("fsdp", "blk"), None, None),
            P("fsdp", None),
            P("fsdp", None),
            P("fsdp", None),
            P("fsdp", None),
            P("fsdp", None),
            P("fsdp"),
            P("fsdp"),
            P("fsdp"),
            P("fsdp"),
        ),
        check_vma=False,
    )
```

profile of v0, /device:TPU:0, one launch (start us, length us, event | category | flops | bytes accessed | tf_op | source)
XLA Modules:
  0.0 524.3 jit_solution(14813867144256259390)
XLA Ops:
  7.3 2.3 constant_dynamic-slice_fusion.4
  17.5 2.7 collective-permute-start.2
  21.2 2.9 pack.1.x_ref
  25.7 15.0 %collective-permute-done.2.refs_1_ = bf16[192,2304]{1,0:T(8,128)(2,1)} collective-permute-done((bf16[192,2304]{1,0:T(8,128)(2,1)}, bf16[192,2304]{1,0:T(8,128)(2,1)}, u32[]{:S(2)}, u32[]{:S(2)}) %collective-permute-start.2) | collective-permute-done | bytes 884768 | tf_op jit(solution)/shard_map/ppermute | solution.py:1272
  49.6 9.5 %qkv.1 = (bf16[1792,2304]{1,0:T(8,128)(2,1)}, bf16[2304,768]{1,0:T(8,128)(2,1)S(1)}) custom-call(s32[24]{0:T(128)S(1)} %copy-done.47, s32[14]{0:T(128)S(1)} %copy-done.70, bf16[1792,768]{1,0:T(8,128)(2,1)S(1)} %copy-done.19, f32[896,128]{1,0:T(8,128)S(1)} %copy-done.13, f32[896,128]{1,0:T(8,128)S(1)} %copy-done.12, bf16[384,2304]{1,0:T(8,128)(2,1)S(1)} %copy-done.46, ...), custom_call_target="tpu_custom_call" | custom-call | flops 5500000256 | tf_op jit(solution)/shard_map/qkv/pallas_call | solution.py:162
  59.1 7.1 %collective-permute-done.5.refs_0_.refs_1_ = bf16[192,768]{1,0:T(8,128)(2,1)S(1)} collective-permute-done((bf16[192,768]{1,0:T(8,128)(2,1)S(1)}, bf16[192,768]{1,0:T(8,128)(2,1)S(1)}, u32[]{:S(2)}, u32[]{:S(2)}) %collective-permute-start.5) | collective-permute-done | bytes 294944 | tf_op jit(solution)/shard_map/ppermute | solution.py:1272
  70.2 3.3 copy-done
  73.6 6.3 %attend.3 = (bf16[1792,768]{1,0:T(8,128)(2,1)S(1)}, f32[6,8,1792]{2,1,0:T(8,128)S(1)}) custom-call(s32[24]{0:T(128)S(1)} %copy-done.47, bf16[1792,2304]{1,0:T(8,128)(2,1)S(1)} %copy-done, bf16[1792,2304]{1,0:T(8,128)(2,1)S(1)} %copy-done, bf16[1792,2304]{1,0:T(8,128)(2,1)S(1)} %copy-done, bf16[192,768]{1,0:T(8,128)(2,1)S(1)} %collective-permute-done.5.refs_0_.refs_1_, ...), custom_call_target="tpu_custom_call" | custom-call | flops 6499999744 | tf_op jit(solution)/shard_map/attend/pallas_call | solution.py:281
  82.0 3.8 collective-permute-done.9.refs_4_.refs_9_
  86.5 6.5 %attend.4 = (bf16[1792,768]{1,0:T(8,128)(2,1)S(1)}, f32[6,8,1792]{2,1,0:T(8,128)S(1)}) custom-call(s32[24]{0:T(128)S(1)} %copy-done.47, bf16[1792,2304]{1,0:T(8,128)(2,1)S(1)} %copy-done, bf16[1792,2304]{1,0:T(8,128)(2,1)S(1)} %copy-done, bf16[1792,2304]{1,0:T(8,128)(2,1)S(1)} %copy-done, ...), custom_call_target="tpu_custom_call", output_to_operand_aliasing={{0}: (4, {}), {1}: (5, {})} | custom-call | flops 6499999744 | tf_op jit(solution)/shard_map/attend/pallas_call | solution.py:281
  93.1 5.0 collective-permute-done.13.refs_5_.refs_14_
  98.1 3.5 collective-permute-done.12.refs_4_.refs_10_
  102.3 6.3 %attend.5 = (bf16[1792,768]{1,0:T(8,128)(2,1)S(1)}, f32[6,8,1792]{2,1,0:T(8,128)S(1)}) custom-call(s32[24]{0:T(128)S(1)} %copy-done.47, bf16[1792,2304]{1,0:T(8,128)(2,1)S(1)} %copy-done, bf16[1792,2304]{1,0:T(8,128)(2,1)S(1)} %copy-done, bf16[1792,2304]{1,0:T(8,128)(2,1)S(1)} %copy-done, ...), custom_call_target="tpu_custom_call", output_to_operand_aliasing={{0}: (4, {}), {1}: (5, {})} | custom-call | flops 6499999744 | tf_op jit(solution)/shard_map/attend/pallas_call | solution.py:281
  110.2 7.1 %collective-permute-done.16.refs_15_ = bf16[384,768]{1,0:T(8,128)(2,1)S(1)} collective-permute-done((bf16[384,768]{1,0:T(8,128)(2,1)S(1)}, bf16[384,768]{1,0:T(8,128)(2,1)S(1)}, u32[]{:S(2)}, u32[]{:S(2)}) %collective-permute-start.16) | collective-permute-done | bytes 589856 | tf_op jit(solution)/shard_map/ppermute | solution.py:1272
  120.1 34.1 %forward.1 = (bf16[1792,768]{1,0:T(8,128)(2,1)}, bf16[1792,768]{1,0:T(8,128)(2,1)}, f32[1792,1]{1,0:T(8,128)}, bf16[1792,9216]{1,0:T(8,128)(2,1)}, bf16[1792,768...) custom-call(s32[24]{0:T(128)S(1)} %copy-done.47, ...), custom_call_target="tpu_custom_call" | custom-call | flops 20999999488 | tf_op jit(solution)/shard_map/forward/pallas_call | solution.py:415
  155.2 5.2 collective-permute-start.19
  161.2 5.3 %collective-permute-start.22 = (bf16[16,512]{1,0:T(8,128)(2,1)S(1)}, bf16[16,512]{1,0:T(8,128)(2,1)S(1)}, u32[]{:S(2)}, u32[]{:S(2)}) collective-permute-start(bf16[16,512]{1,0:T(8,128)(2,1)S(1)} %get-tuple-element.254), channel_id=1, source_target_pairs={{0,18},{1,19},{2,16},{3,17},{4,22},{5,23},{6,20},{7,21},{8,26},{9,... | collective-permute-start | bytes 49160 | tf_op jit(solution)/shard_map/ppermute | solution.py:1272
  167.1 3.2 collective-permute-done.21
  170.3 3.4 collective-permute-start.25
  173.8 4.7 collective-permute-start.24
  190.6 18.8 %ffn_back.3 = (bf16[1792,1536]{1,0:T(8,128)(2,1)}, bf16[2,2,3,192,512]{4,3,2,1,0:T(8,128)(2,1)S(1)}, bf16[2,2,3,192,512]{4,3,2,1,0:T(8,128)(2,1)S(1)}) custom-call(s32[24]{0:T(128)S(1)} %copy-done.47, s32[28]{0:T(128)S(1)} %copy-done.61, s32[28]{0:T(128)S(1)} %copy-done.60, bf16[1792,768]{1,0:T(8,128)(2,1)S(1)} %copy-done.11, ...), custom_call_target="tpu_custom_call" | custom-call | flops 11500000256 | tf_op jit(solution)/shard_map/ffn_back/pallas_call | solution.py:556
  210.5 18.5 %ffn_back.4 = (bf16[1792,1536]{1,0:T(8,128)(2,1)}, bf16[2,2,3,192,512]{4,3,2,1,0:T(8,128)(2,1)S(1)}, bf16[2,2,3,192,512]{4,3,2,1,0:T(8,128)(2,1)}) custom-call(s32[24]{0:T(128)S(1)} %copy-done.47, s32[28]{0:T(128)S(1)} %copy-done.61, s32[28]{0:T(128)S(1)} %copy-done.60, bf16[1792,768]{1,0:T(8,128)(2,1)S(1)} %copy-done.11, ...), custom_call_target="tpu_custom_call" | custom-call | flops 11500000256 | tf_op jit(solution)/shard_map/ffn_back/pallas_call | solution.py:556
  229.0 2.9 collective-permute-start.28
  233.6 19.4 %ffn_back.5 = (bf16[1792,1536]{1,0:T(8,128)(2,1)}, bf16[2,2,3,192,512]{4,3,2,1,0:T(8,128)(2,1)S(1)}, bf16[2,2,3,192,512]{4,3,2,1,0:T(8,128)(2,1)}) custom-call(s32[24]{0:T(128)S(1)} %copy-done.47, s32[28]{0:T(128)S(1)} %copy-done.61, s32[28]{0:T(128)S(1)} %copy-done.60, ...), custom_call_target="tpu_custom_call", output_to_operand_aliasing={{0}: (12, {})} | custom-call | flops 11500000256 | tf_op jit(solution)/shard_map/ffn_back/pallas_call | solution.py:556
  254.4 3.5 collective-permute-start.30
  257.9 4.5 collective-permute-done.27
  264.3 8.0 %collective-permute-start.29 = (bf16[3,192,512]{2,1,0:T(8,128)(2,1)S(1)}, bf16[3,192,512]{2,1,0:T(8,128)(2,1)S(1)}, u32[]{:S(2)}, u32[]{:S(2)}) collective-permute-start(bf16[3,192,512]{2,1,0:T(8,128)(2,1)S(1)} %fusion.11.refs_0_), channel_id=1, source_target_pairs={{0,2},{1,3},{2,0},{3,1},{4,6},{5,7},{6,4},{7,5},{8,10},{9,11},{10,... | collective-permute-start | bytes 1769480 | tf_op jit(solution)/shard_map/ppermute | solution.py:1272
  276.1 2.6 copy-done.10
  281.1 7.5 %norm_one_back.1 = (f32[1792,768]{1,0:T(8,128)S(1)}, bf16[1792,768]{1,0:T(8,128)(2,1)S(1)}, f32[8,768]{1,0:T(8,128)S(1)}, bf16[2,2,96,768]{3,2,1,0:T(8,128)(2,1)S(1)}, bf16[2,2,96,768]{3,2,1,0:T(8,128)(2,1)S(1)}) custom-call(s32[24]{0:T(128)S(1)} %copy-done.48, bf16[1792,1536]{1,0:T(8,128)(2,1)S(1)} %copy-done.10, ...), custom_call_target="tpu_custom_call" | custom-call | flops 6000000000 | tf_op jit(solution)/shard_map/norm_one_back/pallas_call | solution.py:627
  288.7 2.4 copy-done.5
  291.1 3.2 fusion.10.refs_0_
  298.9 7.2 %attend_back.6.refs_0_ = bf16[1792,2304]{1,0:T(8,128)(2,1)} custom-call(s32[24]{0:T(128)S(1)} %copy-done.49, bf16[1792,2304]{1,0:T(8,128)(2,1)} %get-tuple-element.135.q_ref.k_ref.v_ref, bf16[1792,2304]{1,0:T(8,128)(2,1)} %get-tuple-element.135.q_ref.k_ref.v_ref, bf16[1792,2304]{1,0:T(8,128)(2,1)} %get-tuple-element.135.q_ref.k_ref.v_ref, ...), custom_call_target="tpu_custom_call" | custom-call | flops 5500000256 | tf_op jit(solution)/shard_map/attend_back/pallas_call | solution.py:747
  309.4 7.0 %attend_back.7.refs_0_ = bf16[1792,2304]{1,0:T(8,128)(2,1)} custom-call(s32[24]{0:T(128)S(1)} %copy-done.49, bf16[1792,2304]{1,0:T(8,128)(2,1)} %get-tuple-element.135.q_ref.k_ref.v_ref, bf16[1792,2304]{1,0:T(8,128)(2,1)} %get-tuple-element.135.q_ref.k_ref.v_ref, ...), custom_call_target="tpu_custom_call", output_to_operand_aliasing={{}: (9, {})} | custom-call | flops 5500000256 | tf_op jit(solution)/shard_map/attend_back/pallas_call | solution.py:747
  320.1 7.0 %attend_back.8.refs_0_ = bf16[1792,2304]{1,0:T(8,128)(2,1)} custom-call(s32[24]{0:T(128)S(1)} %copy-done.49, bf16[1792,2304]{1,0:T(8,128)(2,1)} %get-tuple-element.135.q_ref.k_ref.v_ref, bf16[1792,2304]{1,0:T(8,128)(2,1)} %get-tuple-element.135.q_ref.k_ref.v_ref, ...), custom_call_target="tpu_custom_call", output_to_operand_aliasing={{}: (9, {})} | custom-call | flops 5500000256 | tf_op jit(solution)/shard_map/attend_back/pallas_call | solution.py:747
  327.1 2.5 fusion.7.refs_2_
  329.6 4.7 collective-permute-start.38
  334.3 10.7 %collective-permute-done.34 = bf16[3,192,512]{2,1,0:T(8,128)(2,1)S(1)} collective-permute-done((bf16[3,192,512]{2,1,0:T(8,128)(2,1)S(1)}, bf16[3,192,512]{2,1,0:T(8,128)(2,1)S(1)}, u32[]{:S(2)}, u32[]{:S(2)}) %collective-permute-start.34) | collective-permute-done | bytes 589856 | tf_op jit(solution)/shard_map/ppermute | solution.py:1298
  345.2 7.2 %attend_back.9.refs_0_ = bf16[1792,2304]{1,0:T(8,128)(2,1)} custom-call(s32[24]{0:T(128)S(1)} %copy-done.49, bf16[1792,2304]{1,0:T(8,128)(2,1)} %get-tuple-element.135.q_ref.k_ref.v_ref, bf16[1792,2304]{1,0:T(8,128)(2,1)} %get-tuple-element.135.q_ref.k_ref.v_ref, ...), custom_call_target="tpu_custom_call", output_to_operand_aliasing={{}: (9, {})} | custom-call | flops 5500000256 | tf_op jit(solution)/shard_map/attend_back/pallas_call | solution.py:747
  352.4 2.5 fusion.6.refs_3_
  354.9 5.8 %collective-permute-start.37 = (bf16[3,192,512]{2,1,0:T(8,128)(2,1)}, bf16[3,192,512]{2,1,0:T(8,128)(2,1)}, u32[]{:S(2)}, u32[]{:S(2)}) collective-permute-start(bf16[3,192,512]{2,1,0:T(8,128)(2,1)} %fusion.6.refs_3_), channel_id=1, source_target_pairs={{0,4},{1,5},{2,6},{3,7},{12,8},{13,9},{14,10},{15,11},{16,20},{17,... | collective-permute-start | bytes 1769480 | tf_op jit(solution)/shard_map/ppermute | solution.py:1298
  360.7 7.2 %qkv_grad.2 = (bf16[2,2,96,2304]{3,2,1,0:T(8,128)(2,1)S(1)}, bf16[2,2,96,2304]{3,2,1,0:T(8,128)(2,1)}) custom-call(s32[24]{0:T(128)S(1)} %copy-done.49, bf16[1792,768]{1,0:T(8,128)(2,1)S(1)} %copy-done.20, bf16[1792,2304]{1,0:T(8,128)(2,1)} %attend_back.9.refs_0_, bf16[2,2,96,768]{3,2,1,0:T(8,128)(2,1)S(1)} %copy-done.66, ...), custom_call_target="tpu_custom_call" | custom-call | flops 4499999744 | tf_op jit(solution)/shard_map/qkv_grad/pallas_call | solution.py:802
  374.9 7.0 %attend_back.10.refs_0_ = bf16[1792,2304]{1,0:T(8,128)(2,1)} custom-call(s32[24]{0:T(128)S(1)} %copy-done.50, bf16[1792,2304]{1,0:T(8,128)(2,1)} %get-tuple-element.135.q_ref.k_ref.v_ref, bf16[1792,2304]{1,0:T(8,128)(2,1)} %get-tuple-element.135.q_ref.k_ref.v_ref, ...), custom_call_target="tpu_custom_call", output_to_operand_aliasing={{}: (9, {})} | custom-call | flops 5500000256 | tf_op jit(solution)/shard_map/attend_back/pallas_call | solution.py:747
  381.9 4.3 collective-permute-done.40
  388.6 2.3 fusion.12.refs_3_
  390.9 7.0 %attend_back.11.refs_0_.refs_2_.refs_3_ = bf16[1792,2304]{1,0:T(8,128)(2,1)} custom-call(s32[24]{0:T(128)S(1)} %copy-done.50, bf16[1792,2304]{1,0:T(8,128)(2,1)} %get-tuple-element.135.q_ref.k_ref.v_ref, bf16[1792,2304]{1,0:T(8,128)(2,1)} %get-tuple-element.135.q_ref.k_ref.v_ref, ...), custom_call_target="tpu_custom_call", output_to_operand_aliasing={{}: (9, {})} | custom-call | flops 5500000256 | tf_op jit(solution)/shard_map/attend_back/pallas_call | solution.py:747
  399.4 12.1 %collective-permute-done.44 = bf16[3,192,512]{2,1,0:T(8,128)(2,1)S(1)} collective-permute-done((bf16[3,192,512]{2,1,0:T(8,128)(2,1)S(1)}, bf16[3,192,512]{2,1,0:T(8,128)(2,1)S(1)}, u32[]{:S(2)}, u32[]{:S(2)}) %collective-permute-start.44) | collective-permute-done | bytes 589856 | tf_op jit(solution)/shard_map/ppermute | solution.py:1298
  414.1 2.9 wide_unfold.2
  417.5 2.6 copy-done.6
  420.0 4.9 qkv_grad.3
  426.5 2.3 collective-permute-start.46
  429.5 5.5 %token_grad.2.refs_5_.refs_0_ = f32[2,768,768]{2,1,0:T(8,128)} custom-call(s32[24]{0:T(128)S(1)} %copy-done.51, f32[1792,768]{1,0:T(8,128)} %copy-done.5, f32[1792,768]{1,0:T(8,128)} %copy-done.5, bf16[1792,2304]{1,0:T(8,128)(2,1)} %attend_back.11.refs_0_.refs_2_.refs_3_, bf16[1792,2304]{1,0:T(8,128)(2,1)} %attend_back.11.refs_0_.refs_2_.refs_3_, ...), custom_call_target="tpu_custom_call" | custom-call | flops 4499999744 | tf_op jit(solution)/shard_map/token_grad/pallas_call | solution.py:882
  435.0 3.4 collective-permute-done.46
  442.7 2.3 copy-done.8
  445.1 7.8 %token_grad.3 = (bf16[768,768]{1,0:T(8,128)(2,1)S(1)}, f32[2,64,768]{2,1,0:T(8,128)}) custom-call(s32[24]{0:T(128)S(1)} %copy-done.51, f32[1792,768]{1,0:T(8,128)} %copy-done.5, f32[1792,768]{1,0:T(8,128)} %copy-done.5, bf16[1792,2304]{1,0:T(8,128)(2,1)} %attend_back.11.refs_0_.refs_2_.refs_3_, bf16[1792,2304]{1,0:T(8,128)(2,1)} %attend_back.11.refs_0_.refs_2_.refs_3_, ...), custom_call_target="tpu_custom_call" | custom-call | flops 4499999744 | tf_op jit(solution)/shard_map/token_grad/pallas_call | solution.py:882
  453.7 3.8 collective-permute-done.53
  462.2 2.6 wide_unfold.3
  467.7 2.3 copy-done.7
  470.0 3.9 place_moved.1.refs_3_
  473.9 9.0 %collective-permute-done.57 = bf16[96,2304]{1,0:T(8,128)(2,1)S(1)} collective-permute-done((bf16[96,2304]{1,0:T(8,128)(2,1)S(1)}, bf16[96,2304]{1,0:T(8,128)(2,1)S(1)}, u32[]{:S(2)}, u32[]{:S(2)}) %collective-permute-start.57) | collective-permute-done | bytes 442400 | tf_op jit(solution)/shard_map/ppermute | solution.py:1298
  485.9 2.4 collective-permute-done.58
  489.8 4.5 collective-permute-start.64
  499.6 2.4 copy-done.9
  501.9 3.3 wide_unfold_parts.1
  505.2 6.7 %all_gather.15 = bf16[384,768]{1,0:T(8,128)(2,1)S(1)} all-gather(bf16[96,768]{1,0:T(8,128)(2,1)S(1)} %broadcast_select_fusion.4), channel_id=1, replica_groups={{0,1,2,3},{4,5,6,7},{8,9,10,11},{12,13,14,15},{16,17,18,19},{20,21,22,2..., dimensions={0}, use_global_device_ids=true | all-gather | bytes 737280 | tf_op jit(solution)/shard_map/all_gather | solution.py:1349
  (343 shorter events, 110.5 us)
Async XLA Ops:
  7.2 405.2 %all-gather.4.cloned.1.call-start = ((), (), s32[]{:S(2)}) async-start(), calls=%async_computation | async-start | bytes 2949120 | tf_op jit(solution)/shard_map/all_gather | solution.py:1349
  17.5 23.1 %collective-permute-start.2 = (bf16[192,2304]{1,0:T(8,128)(2,1)}, bf16[192,2304]{1,0:T(8,128)(2,1)}, u32[]{:S(2)}, u32[]{:S(2)}) collective-permute-start(bf16[192,2304]{1,0:T(8,128)(2,1)} %constant_dynamic-slice_fusion.4), channel_id=1, source_target_pairs={{0,16},{1,17},{2,18},{3,19},{4,20},{5,21},{6,22},{7,23},{8,24},{9,... | collective-permute-start | bytes 2654216 | tf_op jit(solution)/shard_map/ppermute | solution.py:1272
  40.7 5.6 %collective-permute-start.3 = (bf16[192,2304]{1,0:T(8,128)(2,1)}, bf16[192,2304]{1,0:T(8,128)(2,1)S(1)}, u32[]{:S(2)}, u32[]{:S(2)}) collective-permute-start(bf16[192,2304]{1,0:T(8,128)(2,1)} %collective-permute-done.2.refs_1_), channel_id=1, source_target_pairs={{0,1},{1,0},{2,3},{3,2},{4,5},{5,4},{6,7},{7,6},{8,9},{9,8},{10,11... | collective-permute-start | bytes 2654216 | tf_op jit(solution)/shard_map/ppermute | solution.py:1272
  44.1 22.1 %collective-permute-start.6 = (bf16[96,3072]{1,0:T(8,128)(2,1)S(1)}, bf16[96,3072]{1,0:T(8,128)(2,1)S(1)}, u32[]{:S(2)}, u32[]{:S(2)}) collective-permute-start(bf16[96,3072]{1,0:T(8,128)(2,1)S(1)} %constant_dynamic-slice_fusion.2.refs_4_), channel_id=1, source_target_pairs={{0,16},{1,17},{2,18},{3,19},{4,20},{5,21},{6,22},{7,23},{8,24},{9,... | collective-permute-start | bytes 1769480 | tf_op jit(solution)/shard_map/ppermute | solution.py:1272
  46.0 20.3 %collective-permute-start.5 = (bf16[192,768]{1,0:T(8,128)(2,1)S(1)}, bf16[192,768]{1,0:T(8,128)(2,1)S(1)}, u32[]{:S(2)}, u32[]{:S(2)}) collective-permute-start(bf16[192,768]{1,0:T(8,128)(2,1)S(1)} %constant_dynamic-slice_fusion.3.refs_3_), channel_id=1, source_target_pairs={{0,16},{1,17},{2,18},{3,19},{4,20},{5,21},{6,22},{7,23},{8,24},{9,... | collective-permute-start | bytes 884744 | tf_op jit(solution)/shard_map/ppermute | solution.py:1272
  66.2 35.8 %collective-permute-start.10 = (bf16[96,3072]{1,0:T(8,128)(2,1)S(1)}, bf16[96,3072]{1,0:T(8,128)(2,1)S(1)}, u32[]{:S(2)}, u32[]{:S(2)}) collective-permute-start(bf16[96,3072]{1,0:T(8,128)(2,1)S(1)} %collective-permute-done.6.refs_1_.refs_4_), channel_id=1, source_target_pairs={{0,1},{1,0},{2,3},{3,2},{4,5},{5,4},{6,7},{7,6},{8,9},{9,8},{10,11... | collective-permute-start | bytes 1769480 | tf_op jit(solution)/shard_map/ppermute | solution.py:1272
  66.3 15.8 %collective-permute-start.8 = (bf16[96,3072]{1,0:T(8,128)(2,1)S(1)}, bf16[96,3072]{1,0:T(8,128)(2,1)S(1)}, u32[]{:S(2)}, u32[]{:S(2)}) collective-permute-start(bf16[96,3072]{1,0:T(8,128)(2,1)S(1)} %collective-permute-done.6.refs_1_.refs_4_), channel_id=1, source_target_pairs={{0,2},{1,3},{2,0},{3,1},{4,6},{5,7},{6,4},{7,5},{8,10},{9,11},{10,... | collective-permute-start | bytes 1769480 | tf_op jit(solution)/shard_map/ppermute | solution.py:1272
  68.1 11.8 %collective-permute-start.4 = (bf16[4,384]{1,0:T(4,128)(2,1)S(1)}, bf16[4,384]{1,0:T(4,128)(2,1)S(1)}, u32[]{:S(2)}, u32[]{:S(2)}) collective-permute-start(bf16[4,384]{1,0:T(4,128)(2,1)S(1)} %pad_maximum_fusion), channel_id=1, source_target_pairs={{0,16},{1,17},{2,18},{3,19},{4,20},{5,21},{6,22},{7,23},{8,24},{9,... | collective-permute-start | bytes 9224 | tf_op jit(solution)/shard_map/ppermute | solution.py:1272
  69.7 16.6 %collective-permute-start.7 = (bf16[192,768]{1,0:T(8,128)(2,1)S(1)}, bf16[192,768]{1,0:T(8,128)(2,1)S(1)}, u32[]{:S(2)}, u32[]{:S(2)}) collective-permute-start(bf16[192,768]{1,0:T(8,128)(2,1)S(1)} %collective-permute-done.5.refs_0_.refs_1_), channel_id=1, source_target_pairs={{0,1},{1,0},{2,3},{3,2},{4,5},{5,4},{6,7},{7,6},{8,9},{9,8},{10,11... | collective-permute-start | bytes 884744 | tf_op jit(solution)/shard_map/ppermute | solution.py:1272
  69.7 16.1 %collective-permute-start.9 = (bf16[96,3072]{1,0:T(8,128)(2,1)S(1)}, bf16[96,3072]{1,0:T(8,128)(2,1)S(1)}, u32[]{:S(2)}, u32[]{:S(2)}) collective-permute-start(bf16[96,3072]{1,0:T(8,128)(2,1)S(1)} %constant_dynamic-slice_fusion.1.refs_2_), channel_id=1, source_target_pairs={{0,16},{1,17},{2,18},{3,19},{4,20},{5,21},{6,22},{7,23},{8,24},{9,... | collective-permute-start | bytes 1769480 | tf_op jit(solution)/shard_map/ppermute | solution.py:1272
  79.9 18.2 %collective-permute-start.13 = (bf16[384,768]{1,0:T(8,128)(2,1)S(1)}, bf16[384,768]{1,0:T(8,128)(2,1)S(1)}, u32[]{:S(2)}, u32[]{:S(2)}) collective-permute-start(bf16[384,768]{1,0:T(8,128)(2,1)S(1)} %constant_dynamic-slice_fusion.refs_5_), channel_id=1, source_target_pairs={{0,16},{1,17},{2,18},{3,19},{4,20},{5,21},{6,22},{7,23},{8,24},{9,... | collective-permute-start | bytes 1769480 | tf_op jit(solution)/shard_map/ppermute | solution.py:1272
  85.8 31.5 %collective-permute-start.14 = (bf16[96,3072]{1,0:T(8,128)(2,1)S(1)}, bf16[96,3072]{1,0:T(8,128)(2,1)S(1)}, u32[]{:S(2)}, u32[]{:S(2)}) collective-permute-start(bf16[96,3072]{1,0:T(8,128)(2,1)S(1)} %collective-permute-done.9.refs_4_.refs_9_), channel_id=1, source_target_pairs={{0,1},{1,0},{2,3},{3,2},{4,5},{5,4},{6,7},{7,6},{8,9},{9,8},{10,11... | collective-permute-start | bytes 1769480 | tf_op jit(solution)/shard_map/ppermute | solution.py:1272
  85.8 15.7 %collective-permute-start.12 = (bf16[96,3072]{1,0:T(8,128)(2,1)S(1)}, bf16[96,3072]{1,0:T(8,128)(2,1)S(1)}, u32[]{:S(2)}, u32[]{:S(2)}) collective-permute-start(bf16[96,3072]{1,0:T(8,128)(2,1)S(1)} %collective-permute-done.9.refs_4_.refs_9_), channel_id=1, source_target_pairs={{0,2},{1,3},{2,0},{3,1},{4,6},{5,7},{6,4},{7,5},{8,10},{9,11},{10,... | collective-permute-start | bytes 1769480 | tf_op jit(solution)/shard_map/ppermute | solution.py:1272
  86.3 16.0 %collective-permute-start.11 = (bf16[96,3072]{1,0:T(8,128)(2,1)S(1)}, bf16[96,3072]{1,0:T(8,128)(2,1)S(1)}, u32[]{:S(2)}, u32[]{:S(2)}) collective-permute-start(bf16[96,3072]{1,0:T(8,128)(2,1)S(1)} %collective-permute-done.8.refs_3_.refs_5_), channel_id=1, source_target_pairs={{0,1},{1,0},{2,3},{3,2},{4,5},{5,4},{6,7},{7,6},{8,9},{9,8},{10,11... | collective-permute-start | bytes 1769480 | tf_op jit(solution)/shard_map/ppermute | solution.py:1272
  101.5 15.8 %collective-permute-start.17 = (bf16[384,768]{1,0:T(8,128)(2,1)S(1)}, bf16[384,768]{1,0:T(8,128)(2,1)S(1)}, u32[]{:S(2)}, u32[]{:S(2)}) collective-permute-start(bf16[384,768]{1,0:T(8,128)(2,1)S(1)} %collective-permute-done.13.refs_5_.refs_14_), channel_id=1, source_target_pairs={{0,1},{1,0},{2,3},{3,2},{4,5},{5,4},{6,7},{7,6},{8,9},{9,8},{10,11... | collective-permute-start | bytes 1769480 | tf_op jit(solution)/shard_map/ppermute | solution.py:1272
  101.5 15.7 %collective-permute-start.16 = (bf16[384,768]{1,0:T(8,128)(2,1)S(1)}, bf16[384,768]{1,0:T(8,128)(2,1)S(1)}, u32[]{:S(2)}, u32[]{:S(2)}) collective-permute-start(bf16[384,768]{1,0:T(8,128)(2,1)S(1)} %collective-permute-done.13.refs_5_.refs_14_), channel_id=1, source_target_pairs={{0,2},{1,3},{2,0},{3,1},{4,6},{5,7},{6,4},{7,5},{8,10},{9,11},{10,... | collective-permute-start | bytes 1769480 | tf_op jit(solution)/shard_map/ppermute | solution.py:1272
  102.1 15.3 %collective-permute-start.15 = (bf16[96,3072]{1,0:T(8,128)(2,1)S(1)}, bf16[96,3072]{1,0:T(8,128)(2,1)S(1)}, u32[]{:S(2)}, u32[]{:S(2)}) collective-permute-start(bf16[96,3072]{1,0:T(8,128)(2,1)S(1)} %collective-permute-done.12.refs_4_.refs_10_), channel_id=1, source_target_pairs={{0,1},{1,0},{2,3},{3,2},{4,5},{5,4},{6,7},{7,6},{8,9},{9,8},{10,11... | collective-permute-start | bytes 1769480 | tf_op jit(solution)/shard_map/ppermute | solution.py:1272
  155.2 6.1 %collective-permute-start.19 = (bf16[8,512]{1,0:T(8,128)(2,1)S(1)}, bf16[8,512]{1,0:T(8,128)(2,1)S(1)}, u32[]{:S(2)}, u32[]{:S(2)}) collective-permute-start(bf16[8,512]{1,0:T(8,128)(2,1)S(1)} %get-tuple-element.161), channel_id=1, source_target_pairs={{0,1},{1,0},{2,3},{3,2},{4,5},{5,4},{6,7},{7,6},{8,9},{9,8},{10,11... | collective-permute-start | bytes 24584 | tf_op jit(solution)/shard_map/ppermute | solution.py:1272
  161.2 5.9 %collective-permute-start.20 = (bf16[16,512]{1,0:T(8,128)(2,1)S(1)}, bf16[16,512]{1,0:T(8,128)(2,1)S(1)}, u32[]{:S(2)}, u32[]{:S(2)}) collective-permute-start(bf16[16,512]{1,0:T(8,128)(2,1)S(1)} %get-tuple-element.254), channel_id=1, source_target_pairs={{0,16},{1,17},{2,18},{3,19},{4,20},{5,21},{6,22},{7,23},{8,24},{9,... | collective-permute-start | bytes 49160 | tf_op jit(solution)/shard_map/ppermute | solution.py:1272
  161.2 9.1 %collective-permute-start.22 = (bf16[16,512]{1,0:T(8,128)(2,1)S(1)}, bf16[16,512]{1,0:T(8,128)(2,1)S(1)}, u32[]{:S(2)}, u32[]{:S(2)}) collective-permute-start(bf16[16,512]{1,0:T(8,128)(2,1)S(1)} %get-tuple-element.254), channel_id=1, source_target_pairs={{0,18},{1,19},{2,16},{3,17},{4,22},{5,23},{6,20},{7,21},{8,26},{9,... | collective-permute-start | bytes 49160 | tf_op jit(solution)/shard_map/ppermute | solution.py:1272
  170.3 10.8 %collective-permute-start.25 = (bf16[64,512]{1,0:T(8,128)(2,1)S(1)}, bf16[64,512]{1,0:T(8,128)(2,1)S(1)}, u32[]{:S(2)}, u32[]{:S(2)}) collective-permute-start(bf16[64,512]{1,0:T(8,128)(2,1)S(1)} %constant_dynamic-update-slice_fusion.2.refs_0_), channel_id=1, source_target_pairs={{0,12},{1,13},{2,14},{3,15},{4,0},{5,1},{6,2},{7,3},{8,4},{9,5},{1... | collective-permute-start | bytes 196616 | tf_op jit(solution)/shard_map/ppermute | solution.py:1289
  173.8 8.9 %collective-permute-start.24 = (bf16[64,512]{1,0:T(8,128)(2,1)S(1)}, bf16[64,512]{1,0:T(8,128)(2,1)S(1)}, u32[]{:S(2)}, u32[]{:S(2)}) collective-permute-start(bf16[64,512]{1,0:T(8,128)(2,1)S(1)} %constant_dynamic-update-slice_fusion.2.refs_0_), channel_id=1, source_target_pairs={{0,8},{1,9},{2,10},{3,11},{4,12},{5,13},{6,14},{7,15},{8,0},{9,1},... | collective-permute-start | bytes 196616 | tf_op jit(solution)/shard_map/ppermute | solution.py:1289
  178.4 6.1 %collective-permute-start.23 = (bf16[64,512]{1,0:T(8,128)(2,1)S(1)}, bf16[64,512]{1,0:T(8,128)(2,1)S(1)}, u32[]{:S(2)}, u32[]{:S(2)}) collective-permute-start(bf16[64,512]{1,0:T(8,128)(2,1)S(1)} %constant_dynamic-update-slice_fusion.2.refs_0_), channel_id=1, source_target_pairs={{0,4},{1,5},{2,6},{3,7},{4,8},{5,9},{6,10},{7,11},{8,12},{9,13},{1... | collective-permute-start | bytes 196616 | tf_op jit(solution)/shard_map/ppermute | solution.py:1289
  209.4 22.5 %collective-permute-start.26 = (bf16[2,2,3,192,512]{4,3,2,1,0:T(8,128)(2,1)S(1)}, bf16[2,2,3,192,512]{4,3,2,1,0:T(8,128)(2,1)}, u32[]{:S(2)}, u32[]{:S(2)}) collective-permute-start(bf16[2,2,3,192,512]{4,3,2,1,0:T(8,128)(2,1)S(1)} %get-tuple-element.174.refs_9_), channel_id=1, source_target_pairs={{0,1},{1,0},{2,3},{3,2},{4,5},{5,4},{6,7},{7,6},{8,9},{9,8},{10,11... | collective-permute-start | bytes 7077896 | tf_op jit(solution)/shard_map/ppermute | solution.py:1272
  229.0 28.9 %collective-permute-start.28 = (bf16[2,2,3,192,512]{4,3,2,1,0:T(8,128)(2,1)}, bf16[2,2,3,192,512]{4,3,2,1,0:T(8,128)(2,1)}, u32[]{:S(2)}, u32[]{:S(2)}) collective-permute-start(bf16[2,2,3,192,512]{4,3,2,1,0:T(8,128)(2,1)} %get-tuple-element.179.refs_11_), channel_id=1, source_target_pairs={{0,1},{1,0},{2,3},{3,2},{4,5},{5,4},{6,7},{7,6},{8,9},{9,8},{10,11... | collective-permute-start | bytes 7077896 | tf_op jit(solution)/shard_map/ppermute | solution.py:1272
  233.5 28.9 %collective-permute-start.27 = (bf16[2,3,192,512]{3,2,1,0:T(8,128)(2,1)S(1)}, bf16[2,3,192,512]{3,2,1,0:T(8,128)(2,1)}, u32[]{:S(2)}, u32[]{:S(2)}) collective-permute-start(bf16[2,3,192,512]{3,2,1,0:T(8,128)(2,1)S(1)} %fusion.refs_10_), channel_id=1, source_target_pairs={{0,16},{1,17},{2,18},{3,19},{4,20},{5,21},{6,22},{7,23},{8,24},{9,... | collective-permute-start | bytes 3538952 | tf_op jit(solution)/shard_map/ppermute | solution.py:1272
  254.4 41.3 %collective-permute-start.30 = (bf16[2,2,3,192,512]{4,3,2,1,0:T(8,128)(2,1)}, bf16[2,2,3,192,512]{4,3,2,1,0:T(8,128)(2,1)}, u32[]{:S(2)}, u32[]{:S(2)}) collective-permute-start(bf16[2,2,3,192,512]{4,3,2,1,0:T(8,128)(2,1)} %get-tuple-element.189.refs_2_), channel_id=1, source_target_pairs={{0,1},{1,0},{2,3},{3,2},{4,5},{5,4},{6,7},{7,6},{8,9},{9,8},{10,11... | collective-permute-start | bytes 7077896 | tf_op jit(solution)/shard_map/ppermute | solution.py:1272
  264.3 26.8 %collective-permute-start.29 = (bf16[3,192,512]{2,1,0:T(8,128)(2,1)S(1)}, bf16[3,192,512]{2,1,0:T(8,128)(2,1)S(1)}, u32[]{:S(2)}, u32[]{:S(2)}) collective-permute-start(bf16[3,192,512]{2,1,0:T(8,128)(2,1)S(1)} %fusion.11.refs_0_), channel_id=1, source_target_pairs={{0,2},{1,3},{2,0},{3,1},{4,6},{5,7},{6,4},{7,5},{8,10},{9,11},{10,... | collective-permute-start | bytes 1769480 | tf_op jit(solution)/shard_map/ppermute | solution.py:1272
  274.3 42.1 %collective-permute-start.33 = (bf16[2,3,192,512]{3,2,1,0:T(8,128)(2,1)S(1)}, bf16[2,3,192,512]{3,2,1,0:T(8,128)(2,1)}, u32[]{:S(2)}, u32[]{:S(2)}) collective-permute-start(bf16[2,3,192,512]{3,2,1,0:T(8,128)(2,1)S(1)} %fusion.1.refs_1_), channel_id=1, source_target_pairs={{0,16},{1,17},{2,18},{3,19},{4,20},{5,21},{6,22},{7,23},{8,24},{9,... | collective-permute-start | bytes 3538952 | tf_op jit(solution)/shard_map/ppermute | solution.py:1272
  294.3 14.1 %collective-permute-start.31 = (bf16[3,192,512]{2,1,0:T(8,128)(2,1)S(1)}, bf16[3,192,512]{2,1,0:T(8,128)(2,1)S(1)}, u32[]{:S(2)}, u32[]{:S(2)}) collective-permute-start(bf16[3,192,512]{2,1,0:T(8,128)(2,1)S(1)} %fusion.10.refs_0_), channel_id=1, source_target_pairs={{0,4},{1,5},{2,6},{3,7},{12,8},{13,9},{14,10},{15,11},{16,20},{17,... | collective-permute-start | bytes 1769480 | tf_op jit(solution)/shard_map/ppermute | solution.py:1298
  297.4 29.7 %collective-permute-start.35 = (bf16[2,3,192,512]{3,2,1,0:T(8,128)(2,1)S(1)}, bf16[2,3,192,512]{3,2,1,0:T(8,128)(2,1)S(1)}, u32[]{:S(2)}, u32[]{:S(2)}) collective-permute-start(bf16[2,3,192,512]{3,2,1,0:T(8,128)(2,1)S(1)} %fusion.2.refs_1_), channel_id=1, source_target_pairs={{0,2},{1,3},{2,0},{3,1},{4,6},{5,7},{6,4},{7,5},{8,10},{9,11},{10,... | collective-permute-start | bytes 3538952 | tf_op jit(solution)/shard_map/ppermute | solution.py:1272
  308.5 10.1 %collective-permute-start.32 = (bf16[3,192,512]{2,1,0:T(8,128)(2,1)S(1)}, bf16[3,192,512]{2,1,0:T(8,128)(2,1)S(1)}, u32[]{:S(2)}, u32[]{:S(2)}) collective-permute-start(bf16[3,192,512]{2,1,0:T(8,128)(2,1)S(1)} %add_convert_fusion.9.refs_1_), channel_id=1, source_target_pairs={{4,8},{5,9},{6,10},{7,11},{8,4},{9,5},{10,6},{11,7},{20,24},{21,25... | collective-permute-start | bytes 1769480 | tf_op jit(solution)/shard_map/ppermute | solution.py:1298
  317.8 34.5 %collective-permute-start.36 = (bf16[3,192,512]{2,1,0:T(8,128)(2,1)S(1)}, bf16[3,192,512]{2,1,0:T(8,128)(2,1)S(1)}, u32[]{:S(2)}, u32[]{:S(2)}) collective-permute-start(bf16[3,192,512]{2,1,0:T(8,128)(2,1)S(1)} %fusion.8.refs_2_), channel_id=1, source_target_pairs={{0,2},{1,3},{2,0},{3,1},{4,6},{5,7},{6,4},{7,5},{8,10},{9,11},{10,... | collective-permute-start | bytes 1769480 | tf_op jit(solution)/shard_map/ppermute | solution.py:1272
  318.8 26.2 %collective-permute-start.34 = (bf16[3,192,512]{2,1,0:T(8,128)(2,1)S(1)}, bf16[3,192,512]{2,1,0:T(8,128)(2,1)S(1)}, u32[]{:S(2)}, u32[]{:S(2)}) collective-permute-start(bf16[3,192,512]{2,1,0:T(8,128)(2,1)S(1)} %add_convert_fusion.8.refs_1_), channel_id=1, source_target_pairs={{4,0},{5,1},{6,2},{7,3},{8,12},{9,13},{10,14},{11,15},{20,16},{21,... | collective-permute-start | bytes 1769480 | tf_op jit(solution)/shard_map/ppermute | solution.py:1298
  329.6 39.7 %collective-permute-start.38 = (bf16[3,192,512]{2,1,0:T(8,128)(2,1)}, bf16[3,192,512]{2,1,0:T(8,128)(2,1)}, u32[]{:S(2)}, u32[]{:S(2)}) collective-permute-start(bf16[3,192,512]{2,1,0:T(8,128)(2,1)} %fusion.7.refs_2_), channel_id=1, source_target_pairs={{0,16},{1,17},{2,18},{3,19},{4,20},{5,21},{6,22},{7,23},{8,24},{9,... | collective-permute-start | bytes 1769480 | tf_op jit(solution)/shard_map/ppermute | solution.py:1272
  354.9 17.8 %collective-permute-start.37 = (bf16[3,192,512]{2,1,0:T(8,128)(2,1)}, bf16[3,192,512]{2,1,0:T(8,128)(2,1)}, u32[]{:S(2)}, u32[]{:S(2)}) collective-permute-start(bf16[3,192,512]{2,1,0:T(8,128)(2,1)} %fusion.6.refs_3_), channel_id=1, source_target_pairs={{0,4},{1,5},{2,6},{3,7},{12,8},{13,9},{14,10},{15,11},{16,20},{17,... | collective-permute-start | bytes 1769480 | tf_op jit(solution)/shard_map/ppermute | solution.py:1298
  369.2 19.4 %collective-permute-start.41 = (bf16[2,2,96,2304]{3,2,1,0:T(8,128)(2,1)}, bf16[2,2,96,2304]{3,2,1,0:T(8,128)(2,1)}, u32[]{:S(2)}, u32[]{:S(2)}) collective-permute-start(bf16[2,2,96,2304]{3,2,1,0:T(8,128)(2,1)} %get-tuple-element.207.refs_3_), channel_id=1, source_target_pairs={{0,1},{1,0},{2,3},{3,2},{4,5},{5,4},{6,7},{7,6},{8,9},{9,8},{10,11... | collective-permute-start | bytes 5308424 | tf_op jit(solution)/shard_map/ppermute | solution.py:1272
  369.2 91.3 %all-gather.6.cloned.1.call-start = ((), (), s32[]{:S(2)}) async-start(), calls=%async_computation.1 | async-start | bytes 2949120 | tf_op jit(solution)/shard_map/all_gather | solution.py:1349
  371.4 14.8 %collective-permute-start.40 = (bf16[3,192,512]{2,1,0:T(8,128)(2,1)S(1)}, bf16[3,192,512]{2,1,0:T(8,128)(2,1)S(1)}, u32[]{:S(2)}, u32[]{:S(2)}) collective-permute-start(bf16[3,192,512]{2,1,0:T(8,128)(2,1)S(1)} %fusion.4.refs_2_), channel_id=1, source_target_pairs={{0,4},{1,5},{2,6},{3,7},{12,8},{13,9},{14,10},{15,11},{16,20},{17,... | collective-permute-start | bytes 1769480 | tf_op jit(solution)/shard_map/ppermute | solution.py:1298
  374.1 12.9 %collective-permute-start.39 = (bf16[3,192,512]{2,1,0:T(8,128)(2,1)S(1)}, bf16[3,192,512]{2,1,0:T(8,128)(2,1)S(1)}, u32[]{:S(2)}, u32[]{:S(2)}) collective-permute-start(bf16[3,192,512]{2,1,0:T(8,128)(2,1)S(1)} %add_convert_fusion.7.refs_1_), channel_id=1, source_target_pairs={{4,8},{5,9},{6,10},{7,11},{8,4},{9,5},{10,6},{11,7},{20,24},{21,25... | collective-permute-start | bytes 1769480 | tf_op jit(solution)/shard_map/ppermute | solution.py:1298
  386.4 11.5 %collective-permute-start.42 = (bf16[3,192,512]{2,1,0:T(8,128)(2,1)S(1)}, bf16[3,192,512]{2,1,0:T(8,128)(2,1)S(1)}, u32[]{:S(2)}, u32[]{:S(2)}) collective-permute-start(bf16[3,192,512]{2,1,0:T(8,128)(2,1)S(1)} %add_convert_fusion.5.refs_2_), channel_id=1, source_target_pairs={{4,8},{5,9},{6,10},{7,11},{8,4},{9,5},{10,6},{11,7},{20,24},{21,25... | collective-permute-start | bytes 1769480 | tf_op jit(solution)/shard_map/ppermute | solution.py:1298
  387.2 24.2 %collective-permute-start.44 = (bf16[3,192,512]{2,1,0:T(8,128)(2,1)S(1)}, bf16[3,192,512]{2,1,0:T(8,128)(2,1)S(1)}, u32[]{:S(2)}, u32[]{:S(2)}) collective-permute-start(bf16[3,192,512]{2,1,0:T(8,128)(2,1)S(1)} %add_convert_fusion.6.refs_1_), channel_id=1, source_target_pairs={{4,0},{5,1},{6,2},{7,3},{8,12},{9,13},{10,14},{11,15},{20,16},{21,... | collective-permute-start | bytes 1769480 | tf_op jit(solution)/shard_map/ppermute | solution.py:1298
  390.8 34.1 %collective-permute-start.45 = (bf16[2,96,2304]{2,1,0:T(8,128)(2,1)}, bf16[2,96,2304]{2,1,0:T(8,128)(2,1)}, u32[]{:S(2)}, u32[]{:S(2)}) collective-permute-start(bf16[2,96,2304]{2,1,0:T(8,128)(2,1)} %fusion.12.refs_3_), channel_id=1, source_target_pairs={{0,2},{1,3},{2,0},{3,1},{4,6},{5,7},{6,4},{7,5},{8,10},{9,11},{10,... | collective-permute-start | bytes 2654216 | tf_op jit(solution)/shard_map/ppermute | solution.py:1272
  398.1 26.9 %collective-permute-start.43 = (bf16[3,192,512]{2,1,0:T(8,128)(2,1)S(1)}, bf16[3,192,512]{2,1,0:T(8,128)(2,1)S(1)}, u32[]{:S(2)}, u32[]{:S(2)}) collective-permute-start(bf16[3,192,512]{2,1,0:T(8,128)(2,1)S(1)} %add_convert_fusion.4.refs_2_), channel_id=1, source_target_pairs={{4,0},{5,1},{6,2},{7,3},{8,12},{9,13},{10,14},{11,15},{20,16},{21,... | collective-permute-start | bytes 1769480 | tf_op jit(solution)/shard_map/ppermute | solution.py:1298
  412.4 99.6 %all-gather.8.cloned.1.call-start = ((), (), s32[]{:S(2)}) async-start(), calls=%async_computation.2 | async-start | bytes 2211840 | tf_op jit(solution)/shard_map/all_gather | solution.py:1349
  426.5 11.9 %collective-permute-start.46 = (bf16[96,2304]{1,0:T(8,128)(2,1)S(1)}, bf16[96,2304]{1,0:T(8,128)(2,1)S(1)}, u32[]{:S(2)}, u32[]{:S(2)}) collective-permute-start(bf16[96,2304]{1,0:T(8,128)(2,1)S(1)} %fusion.15.refs_6_), channel_id=1, source_target_pairs={{0,16},{1,17},{2,18},{3,19},{4,20},{5,21},{6,22},{7,23},{8,24},{9,... | collective-permute-start | bytes 1327112 | tf_op jit(solution)/shard_map/ppermute | solution.py:1272
  428.9 6.1 %collective-permute-start.48 = (f32[8,768]{1,0:T(8,128)S(1)}, f32[8,768]{1,0:T(8,128)S(1)}, u32[]{:S(2)}, u32[]{:S(2)}) collective-permute-start(f32[8,768]{1,0:T(8,128)S(1)} %copy-done.55), channel_id=1, source_target_pairs={{0,1},{1,0},{2,3},{3,2},{4,5},{5,4},{6,7},{7,6},{8,9},{9,8},{10,11... | collective-permute-start | bytes 73736 | tf_op jit(solution)/shard_map/ppermute | solution.py:1272
  429.0 28.6 %collective-permute-start.50 = (bf16[3,192,512]{2,1,0:T(8,128)(2,1)S(1)}, bf16[3,192,512]{2,1,0:T(8,128)(2,1)S(1)}, u32[]{:S(2)}, u32[]{:S(2)}) collective-permute-start(bf16[3,192,512]{2,1,0:T(8,128)(2,1)S(1)} %broadcast_select_fusion.refs_5_.p00), channel_id=1, source_target_pairs={{0,2},{1,3},{2,0},{3,1},{4,6},{5,7},{6,4},{7,5},{8,10},{9,11},{10,... | collective-permute-start | bytes 1769480 | tf_op jit(solution)/shard_map/ppermute | solution.py:1272
  429.0 12.1 %collective-permute-start.47 = (bf16[2,2,96,768]{3,2,1,0:T(8,128)(2,1)S(1)}, bf16[2,2,96,768]{3,2,1,0:T(8,128)(2,1)S(1)}, u32[]{:S(2)}, u32[]{:S(2)}) collective-permute-start(bf16[2,2,96,768]{3,2,1,0:T(8,128)(2,1)S(1)} %get-tuple-element.219.refs_7_), channel_id=1, source_target_pairs={{0,1},{1,0},{2,3},{3,2},{4,5},{5,4},{6,7},{7,6},{8,9},{9,8},{10,11... | collective-permute-start | bytes 1769480 | tf_op jit(solution)/shard_map/ppermute | solution.py:1272
  439.8 13.0 %collective-permute-start.51 = (bf16[96,2304]{1,0:T(8,128)(2,1)S(1)}, bf16[96,2304]{1,0:T(8,128)(2,1)S(1)}, u32[]{:S(2)}, u32[]{:S(2)}) collective-permute-start(bf16[96,2304]{1,0:T(8,128)(2,1)S(1)} %fusion.14.refs_6_), channel_id=1, source_target_pairs={{0,4},{1,5},{2,6},{3,7},{12,8},{13,9},{14,10},{15,11},{16,20},{17,... | collective-permute-start | bytes 1327112 | tf_op jit(solution)/shard_map/ppermute | solution.py:1298
  441.2 18.5 %collective-permute-start.52 = (bf16[2,96,768]{2,1,0:T(8,128)(2,1)S(1)}, bf16[2,96,768]{2,1,0:T(8,128)(2,1)S(1)}, u32[]{:S(2)}, u32[]{:S(2)}) collective-permute-start(bf16[2,96,768]{2,1,0:T(8,128)(2,1)S(1)} %fusion.16.refs_7_), channel_id=1, source_target_pairs={{0,16},{1,17},{2,18},{3,19},{4,20},{5,21},{6,22},{7,23},{8,24},{9,... | collective-permute-start | bytes 884744 | tf_op jit(solution)/shard_map/ppermute | solution.py:1272
  452.9 11.8 %collective-permute-start.54 = (bf16[96,2304]{1,0:T(8,128)(2,1)S(1)}, bf16[96,2304]{1,0:T(8,128)(2,1)S(1)}, u32[]{:S(2)}, u32[]{:S(2)}) collective-permute-start(bf16[96,2304]{1,0:T(8,128)(2,1)S(1)} %add_convert_fusion.11.refs_4_), channel_id=1, source_target_pairs={{4,8},{5,9},{6,10},{7,11},{8,4},{9,5},{10,6},{11,7},{20,24},{21,25... | collective-permute-start | bytes 1327112 | tf_op jit(solution)/shard_map/ppermute | solution.py:1298
  453.6 3.9 collective-permute-start.53
  457.5 10.1 %collective-permute-start.49 = (bf16[768,768]{1,0:T(8,128)(2,1)S(1)}, bf16[768,768]{1,0:T(8,128)(2,1)}, u32[]{:S(2)}, u32[]{:S(2)}) collective-permute-start(bf16[768,768]{1,0:T(8,128)(2,1)S(1)} %get-tuple-element.225.own_ref), channel_id=1, source_target_pairs={{0,1},{1,0},{2,3},{3,2},{4,5},{5,4},{6,7},{7,6},{8,9},{9,8},{10,11... | collective-permute-start | bytes 3538952 | tf_op jit(solution)/shard_map/ppermute | solution.py:1272
  457.6 8.6 %collective-permute-start.56 = (f32[8,768]{1,0:T(8,128)S(1)}, f32[8,768]{1,0:T(8,128)S(1)}, u32[]{:S(2)}, u32[]{:S(2)}) collective-permute-start(f32[8,768]{1,0:T(8,128)S(1)} %add.255.refs_6_), channel_id=1, source_target_pairs={{0,2},{1,3},{2,0},{3,1},{4,6},{5,7},{6,4},{7,5},{8,10},{9,11},{10,... | collective-permute-start | bytes 73736 | tf_op jit(solution)/shard_map/ppermute | solution.py:1272
  460.5 6.0 %collective-permute-start.55 = (bf16[96,768]{1,0:T(8,128)(2,1)S(1)}, bf16[96,768]{1,0:T(8,128)(2,1)}, u32[]{:S(2)}, u32[]{:S(2)}) collective-permute-start(bf16[96,768]{1,0:T(8,128)(2,1)S(1)} %fusion.19.refs_5_), channel_id=1, source_target_pairs={{0,2},{1,3},{2,0},{3,1},{4,6},{5,7},{6,4},{7,5},{8,10},{9,11},{10,... | collective-permute-start | bytes 442376 | tf_op jit(solution)/shard_map/ppermute | solution.py:1272
  464.9 18.0 %collective-permute-start.57 = (bf16[96,2304]{1,0:T(8,128)(2,1)S(1)}, bf16[96,2304]{1,0:T(8,128)(2,1)S(1)}, u32[]{:S(2)}, u32[]{:S(2)}) collective-permute-start(bf16[96,2304]{1,0:T(8,128)(2,1)S(1)} %add_convert_fusion.10.refs_2_), channel_id=1, source_target_pairs={{4,0},{5,1},{6,2},{7,3},{8,12},{9,13},{10,14},{11,15},{20,16},{21,... | collective-permute-start | bytes 1327112 | tf_op jit(solution)/shard_map/ppermute | solution.py:1298
  483.7 4.6 collective-permute-start.58
  485.3 14.2 %collective-permute-start.61 = (bf16[3,192,512]{2,1,0:T(8,128)(2,1)S(1)}, bf16[3,192,512]{2,1,0:T(8,128)(2,1)S(1)}, u32[]{:S(2)}, u32[]{:S(2)}) collective-permute-start(bf16[3,192,512]{2,1,0:T(8,128)(2,1)S(1)} %broadcast_select_fusion.refs_5_.p00), channel_id=1, source_target_pairs={{0,1},{1,0},{2,3},{3,2},{4,5},{5,4},{6,7},{7,6},{8,9},{9,8},{10,11... | collective-permute-start | bytes 1769480 | tf_op jit(solution)/shard_map/ppermute | solution.py:1272
  485.4 14.1 %collective-permute-start.62 = (bf16[3,192,512]{2,1,0:T(8,128)(2,1)S(1)}, bf16[3,192,512]{2,1,0:T(8,128)(2,1)S(1)}, u32[]{:S(2)}, u32[]{:S(2)}) collective-permute-start(bf16[3,192,512]{2,1,0:T(8,128)(2,1)S(1)} %collective-permute-done.50.refs_3_.p01), channel_id=1, source_target_pairs={{0,1},{1,0},{2,3},{3,2},{4,5},{5,4},{6,7},{7,6},{8,9},{9,8},{10,11... | collective-permute-start | bytes 1769480 | tf_op jit(solution)/shard_map/ppermute | solution.py:1272
  485.9 3.8 collective-permute-start.63
  488.3 9.2 %collective-permute-start.59 = (bf16[96,768]{1,0:T(8,128)(2,1)S(1)}, bf16[96,768]{1,0:T(8,128)(2,1)S(1)}, u32[]{:S(2)}, u32[]{:S(2)}) collective-permute-start(bf16[96,768]{1,0:T(8,128)(2,1)S(1)} %add_convert_fusion.14.refs_5_), channel_id=1, source_target_pairs={{4,8},{5,9},{6,10},{7,11},{8,4},{9,5},{10,6},{11,7},{20,24},{21,25... | collective-permute-start | bytes 442376 | tf_op jit(solution)/shard_map/ppermute | solution.py:1298
  489.8 7.8 %collective-permute-start.64 = (f32[8,768]{1,0:T(8,128)S(1)}, f32[8,768]{1,0:T(8,128)S(1)}, u32[]{:S(2)}, u32[]{:S(2)}) collective-permute-start(f32[8,768]{1,0:T(8,128)S(1)} %add.264.refs_6_), channel_id=1, source_target_pairs={{0,8},{1,9},{2,10},{3,11},{4,12},{5,13},{6,14},{7,15},{8,0},{9,1},... | collective-permute-start | bytes 73736 | tf_op jit(solution)/shard_map/ppermute | solution.py:1272
  497.6 7.6 %collective-permute-start.60 = (bf16[96,768]{1,0:T(8,128)(2,1)S(1)}, bf16[96,768]{1,0:T(8,128)(2,1)S(1)}, u32[]{:S(2)}, u32[]{:S(2)}) collective-permute-start(bf16[96,768]{1,0:T(8,128)(2,1)S(1)} %add_convert_fusion.13), channel_id=1, source_target_pairs={{4,0},{5,1},{6,2},{7,3},{8,12},{9,13},{10,14},{11,15},{20,16},{21,... | collective-permute-start | bytes 442376 | tf_op jit(solution)/shard_map/ppermute | solution.py:1298
  (91 other events, 785.8 us)
Sparse Core Ops, SparseCore 0:
  369.3 29.5 all-gather.3
  412.5 28.1 all-gather.5
  483.9 18.8 all-gather.7
where the time goes:
time: 529 us; the launch traced here: 524 us
  Pallas kernels  215 us (41%)
  waiting for transfers between devices  107 us (20%)
  starting transfers between devices  91.8 us (17%)
  local copies, waits for them, and re-layouts  52.5 us (10%)
  other arithmetic  33.3 us (6%)
  between operations  18.1 us (3%)
  blocking collectives  6.69 us (1%)
    ppermute x47, waiting for transfers between devices, swap(): return lax.ppermute(value, AXES, pairs)  62.9 us
    ppermute x47, starting transfers between devices, swap(): return lax.ppermute(value, AXES, pairs)  60 us
    pallas_call x3, Pallas kernels, ffn_back(): pl.pallas_call(functools.partial(ffn_back_kernel, starts), grid_spec=grid...  56.7 us
    unnamed x182, local copies, waits for them, and re-layouts  42.6 us
    pallas_call x6, Pallas kernels, attend_back(): pl.pallas_call(attend_back_kernel, grid_spec=grid_spec, out_shape=jax.Sha...  42.4 us
    ppermute x15, waiting for transfers between devices, step(): return lax.ppermute(value, AXES, pairs)  40.8 us
    pallas_call x1, Pallas kernels, forward(): pl.pallas_call(forward_kernel, grid_spec=grid_spec, out_shape=[array(widt...  34.1 us
    convert_element_type x25, other arithmetic, stages(): add = lambda *terms: sum((term.astype(F32) for term in terms)).astype(BF16)  27.7 us
  transfers between devices with their start and end apart: 68, of which 26 were waited for; matrix products, arithmetic and copies ran while one was open for 7% of the time, Pallas kernels for 30%

commit v1 on v0

--- a/solution.py
+++ b/solution.py
@@ -302,7 +302,7 @@
     meta, counts, att_ref, x_ref, gain_ref, bias_ref, *refs,
 ):
     outs, scratch = refs[-18:-7], refs[-7:]
-    pieces = [refs[0:3], refs[3:8], refs[8:13], refs[13:18]]
+    pieces = [refs[0:3], refs[3:8], refs[8:13], refs[13:16]]
     low_ref, z1_ref, r1_ref, saved_ref, z2_ref, r2_ref, sums_ref = outs[:7]
     whole_outs = outs[7:]
     wholes, (sems, out_sems) = scratch[:4], scratch[5:]
@@ -399,7 +399,7 @@
         grid=(rows // TILE,),
         in_specs=[tiled(width), tiled(width)]
         + [resident(gain.shape), resident(bias.shape)]
-        + anywhere(18 + len(after)),
+        + anywhere(16 + len(after)),
         out_specs=[
             tiled(width), tiled(width), tiled(1), tiled(3 * inner), tiled(width), tiled(1),
             pl.BlockSpec((8, width), lambda i, m, *_: (live(i, m), 0)),
@@ -1439,7 +1439,6 @@
     got_qkv = tie(got_qkv, x)
     pieces_qkv = (combined_projection_matrix, got_qkv, links.core(got_qkv))
     qkv, wqkv = project(meta, table_block, x, pieces_qkv, tables, (part_out, part_gate))
-    got_out, got_gate = tie((got_out, got_gate), qkv)
     own_vectors = tie(
         (initial_layernorm_scale, initial_layernorm_shift, later_layernorm_scale, later_layernorm_shift),
         qkv,
@@ -1451,26 +1450,23 @@
     ).astype(F32)
     gain_one, bias_one, gain_two, bias_two = (vectors[at : at + 1] for at in range(4))
     part_up = tie(part_of(widening_matrix, 4, quarter), qkv)
-    far_out, along_gate, got_up = links.core(got_out), links.row(got_gate), links.side(part_up)
-    heads = attend(meta, qkv, 0, 2, (), (got_out, got_gate, part_up))
+    got_up = links.side(part_up)
+    heads = attend(meta, qkv, 0, 2, (), (part_up,))
+    got_out, got_gate = tie((got_out, got_gate), heads[1])
+    part_down = tie(part_of(narrowing_matrix, 2, core), heads[1])
+    far_out, along_gate, got_down = links.core(got_out), links.row(got_gate), links.side(part_down)
+    heads = attend(meta, qkv, 1, 2, heads, (got_out, got_gate, part_down))
     along_gate, got_up = tie((along_gate, got_up), heads[1])
-    part_down = tie(part_of(narrowing_matrix, 4, quarter), heads[1])
     far_gate = links.core(got_gate), links.core(along_gate)
-    along_up, got_down = links.row(got_up), links.side(part_down)
-    heads = attend(meta, qkv, 1, 2, heads, (far_out, along_gate, got_up, part_down))
-    along_up, got_down = tie((along_up, got_down), heads[1])
-    far_up = links.core(got_up), links.core(along_up)
-    along_down = links.row(got_down)
-    att, lse = attend(
-        meta, qkv, 2, 2, heads, (*far_gate, along_up, got_down, vectors)
-    )
-    along_down = tie(along_down, lse)
-    far_down = links.core(got_down), links.core(along_down)
+    along_up = links.row(got_up)
+    att, lse = attend(meta, qkv, 2, 2, heads, (far_out, along_gate, got_up, vectors))
+    along_up, got_down = tie((along_up, got_down), lse)
+    far_up, far_down = (links.core(got_up), links.core(along_up)), links.core(got_down)
     weights = [
         (mixing_result_matrix, got_out, far_out),
         (gating_matrix, got_gate, along_gate, *far_gate),
         (widening_matrix, got_up, along_up, *far_up),
-        (narrowing_matrix, got_down, along_down, *far_down),
+        (narrowing_matrix, got_down, far_down),
     ]
     low, z1, r1, saved, z2, r2, sums, wo, wg, wu, wd = forward(
         meta, counts, att, x, weights, gain_one, bias_one

time: 529 us -> 516 us (0.975)
  waiting for transfers between devices: 107 us -> 77.7 us
  Pallas kernels: 215 us -> 244 us
  starting transfers between devices: 91.8 us -> 84.3 us
    ppermute x15, waiting for transfers between devices: 40.8 us -> 22.4 us  [step(): return lax.ppermute(value, AXES, pairs)]
    ppermute x47 -> x45, waiting for transfers between devices: 62.9 us -> 50.6 us  [swap(): return lax.ppermute(value, AXES, pairs)]
    pallas_call x3, Pallas kernels: 56.7 us -> 64.9 us  [ffn_back(): pl.pallas_call(functools.partial(ffn_back_kernel, starts), grid_spec=grid...]
    ppermute x3, starting transfers between devices: 10.1 us -> 2.02 us  [shift(): return lax.ppermute(value, AXES, pairs)]
    pallas_call x6, Pallas kernels: 42.4 us -> 49.6 us  [attend_back(): pl.pallas_call(attend_back_kernel, grid_spec=grid_spec, out_shape=jax.Sha...]
    unnamed x182 -> x188, local copies, waits for them, and re-layouts: 42.6 us -> 38.2 us
    ppermute x47 -> x45, starting transfers between devices: 60 us -> 60.4 us  [swap(): return lax.ppermute(value, AXES, pairs)]
  transfers between devices with their start and end apart: 68 -> 66, of which waited for: 26 -> 26; matrix products, arithmetic and copies ran while one was open for 7% -> 7% of each run, Pallas kernels for 30% -> 35%
where the time goes in v1:
time: 516 us; the launch traced here: 512 us
  Pallas kernels  244 us (47%)
  starting transfers between devices  84.3 us (16%)
  waiting for transfers between devices  77.7 us (15%)
  local copies, waits for them, and re-layouts  47.4 us (9%)
  other arithmetic  33.2 us (6%)
  between operations  18.3 us (4%)
  blocking collectives  6.69 us (1%)
    pallas_call x3, Pallas kernels, ffn_back(): pl.pallas_call(functools.partial(ffn_back_kernel, starts), grid_spec=grid...  64.9 us
    ppermute x45, starting transfers between devices, swap(): return lax.ppermute(value, AXES, pairs)  60.4 us
    ppermute x45, waiting for transfers between devices, swap(): return lax.ppermute(value, AXES, pairs)  50.6 us
    pallas_call x6, Pallas kernels, attend_back(): pl.pallas_call(attend_back_kernel, grid_spec=grid_spec, out_shape=jax.Sha...  49.6 us
    pallas_call x1, Pallas kernels, forward(): pl.pallas_call(forward_kernel, grid_spec=grid_spec, out_shape=[array(widt...  39.2 us
    unnamed x188, local copies, waits for them, and re-layouts  38.2 us
    convert_element_type x25, other arithmetic, stages(): add = lambda *terms: sum((term.astype(F32) for term in terms)).astype(BF16)  27.6 us
    ppermute x15, waiting for transfers between devices, step(): return lax.ppermute(value, AXES, pairs)  22.4 us
  transfers between devices with their start and end apart: 66, of which 26 were waited for; matrix products, arithmetic and copies ran while one was open for 7% of the time, Pallas kernels for 35%

profile of v1, /device:TPU:0, one launch (start us, length us, event | category | flops | bytes accessed | tf_op | source)
XLA Modules:
  0.0 511.8 jit_solution(3141340958562822898)
XLA Ops:
  7.3 2.3 constant_dynamic-slice_fusion.4
  16.6 2.7 collective-permute-start.2
  19.3 3.2 pack.1.x_ref
  22.5 17.2 %collective-permute-done.2.refs_1_ = bf16[192,2304]{1,0:T(8,128)(2,1)} collective-permute-done((bf16[192,2304]{1,0:T(8,128)(2,1)}, bf16[192,2304]{1,0:T(8,128)(2,1)}, u32[]{:S(2)}, u32[]{:S(2)}) %collective-permute-start.2) | collective-permute-done | bytes 884768 | tf_op jit(solution)/shard_map/ppermute | solution.py:1272
  45.7 10.9 %qkv.1 = (bf16[1792,2304]{1,0:T(8,128)(2,1)}, bf16[2304,768]{1,0:T(8,128)(2,1)S(1)}) custom-call(s32[24]{0:T(128)S(1)} %copy-done.45, s32[14]{0:T(128)S(1)} %copy-done.69, bf16[1792,768]{1,0:T(8,128)(2,1)S(1)} %pack.1.x_ref, f32[896,128]{1,0:T(8,128)S(1)} %copy-done.13, f32[896,128]{1,0:T(8,128)S(1)} %copy-done.12, bf16[384,2304]{1,0:T(8,128)(2,1)S(1)} %copy-done.42, ...), custom_call_target="tpu_custom_call" | custom-call | flops 5500000256 | tf_op jit(solution)/shard_map/qkv/pallas_call | solution.py:162
  56.6 3.0 collective-permute-start.9
  59.6 3.3 copy-done
  63.0 7.3 %attend.3 = (bf16[1792,768]{1,0:T(8,128)(2,1)S(1)}, f32[6,8,1792]{2,1,0:T(8,128)S(1)}) custom-call(s32[24]{0:T(128)S(1)} %copy-done.45, bf16[1792,2304]{1,0:T(8,128)(2,1)S(1)} %copy-done, bf16[1792,2304]{1,0:T(8,128)(2,1)S(1)} %copy-done, bf16[1792,2304]{1,0:T(8,128)(2,1)S(1)} %copy-done, bf16[96,3072]{1,0:T(8,128)(2,1)S(1)} %constant_dynamic-slice_fusion.1.refs_0_), custom_call_target="tpu_custom_call" | custom-call | flops 6499999744 | tf_op jit(solution)/shard_map/attend/pallas_call | solution.py:281
  70.3 3.1 collective-permute-start.4
  75.2 7.5 %attend.4 = (bf16[1792,768]{1,0:T(8,128)(2,1)S(1)}, f32[6,8,1792]{2,1,0:T(8,128)S(1)}) custom-call(s32[24]{0:T(128)S(1)} %copy-done.45, bf16[1792,2304]{1,0:T(8,128)(2,1)S(1)} %copy-done, bf16[1792,2304]{1,0:T(8,128)(2,1)S(1)} %copy-done, bf16[1792,2304]{1,0:T(8,128)(2,1)S(1)} %copy-done, ...), custom_call_target="tpu_custom_call", output_to_operand_aliasing={{0}: (4, {}), {1}: (5, {})} | custom-call | flops 6499999744 | tf_op jit(solution)/shard_map/attend/pallas_call | solution.py:281
  82.7 7.4 %collective-permute-done.8.refs_3_.refs_5_ = bf16[96,3072]{1,0:T(8,128)(2,1)S(1)} collective-permute-done((bf16[96,3072]{1,0:T(8,128)(2,1)S(1)}, bf16[96,3072]{1,0:T(8,128)(2,1)S(1)}, u32[]{:S(2)}, u32[]{:S(2)}) %collective-permute-start.8) | collective-permute-done | bytes 589856 | tf_op jit(solution)/shard_map/ppermute | solution.py:1272
  90.5 7.2 %attend.5 = (bf16[1792,768]{1,0:T(8,128)(2,1)S(1)}, f32[6,8,1792]{2,1,0:T(8,128)S(1)}) custom-call(s32[24]{0:T(128)S(1)} %copy-done.45, bf16[1792,2304]{1,0:T(8,128)(2,1)S(1)} %copy-done, bf16[1792,2304]{1,0:T(8,128)(2,1)S(1)} %copy-done, bf16[1792,2304]{1,0:T(8,128)(2,1)S(1)} %copy-done, ...), custom_call_target="tpu_custom_call", output_to_operand_aliasing={{0}: (4, {}), {1}: (5, {})} | custom-call | flops 6499999744 | tf_op jit(solution)/shard_map/attend/pallas_call | solution.py:281
  99.3 5.4 %collective-permute-done.12.refs_10_ = bf16[96,3072]{1,0:T(8,128)(2,1)S(1)} collective-permute-done((bf16[96,3072]{1,0:T(8,128)(2,1)S(1)}, bf16[96,3072]{1,0:T(8,128)(2,1)S(1)}, u32[]{:S(2)}, u32[]{:S(2)}) %collective-permute-start.12) | collective-permute-done | bytes 589856 | tf_op jit(solution)/shard_map/ppermute | solution.py:1272
  105.9 2.6 collective-permute-done.10.refs_6_
  112.2 39.2 %forward.1 = (bf16[1792,768]{1,0:T(8,128)(2,1)}, bf16[1792,768]{1,0:T(8,128)(2,1)}, f32[1792,1]{1,0:T(8,128)}, bf16[1792,9216]{1,0:T(8,128)(2,1)}, bf16[1792,768...) custom-call(s32[24]{0:T(128)S(1)} %copy-done.45, ...), custom_call_target="tpu_custom_call" | custom-call | flops 20999999488 | tf_op jit(solution)/shard_map/forward/pallas_call | solution.py:415
  153.5 10.3 %collective-permute-start.18 = (bf16[16,512]{1,0:T(8,128)(2,1)S(1)}, bf16[16,512]{1,0:T(8,128)(2,1)S(1)}, u32[]{:S(2)}, u32[]{:S(2)}) collective-permute-start(bf16[16,512]{1,0:T(8,128)(2,1)S(1)} %get-tuple-element.252), channel_id=1, source_target_pairs={{0,16},{1,17},{2,18},{3,19},{4,20},{5,21},{6,22},{7,23},{8,24},{9,... | collective-permute-start | bytes 49160 | tf_op jit(solution)/shard_map/ppermute | solution.py:1272
  165.5 2.2 collective-permute-done.19
  181.9 21.7 %ffn_back.3 = (bf16[1792,1536]{1,0:T(8,128)(2,1)}, bf16[2,2,3,192,512]{4,3,2,1,0:T(8,128)(2,1)S(1)}, bf16[2,2,3,192,512]{4,3,2,1,0:T(8,128)(2,1)S(1)}) custom-call(s32[24]{0:T(128)S(1)} %copy-done.45, s32[28]{0:T(128)S(1)} %copy-done.60, s32[28]{0:T(128)S(1)} %copy-done.59, bf16[1792,768]{1,0:T(8,128)(2,1)S(1)} %copy-done.11, ...), custom_call_target="tpu_custom_call" | custom-call | flops 11500000256 | tf_op jit(solution)/shard_map/ffn_back/pallas_call | solution.py:556
  203.6 21.3 %ffn_back.4 = (bf16[1792,1536]{1,0:T(8,128)(2,1)}, bf16[2,2,3,192,512]{4,3,2,1,0:T(8,128)(2,1)S(1)}, bf16[2,2,3,192,512]{4,3,2,1,0:T(8,128)(2,1)}) custom-call(s32[24]{0:T(128)S(1)} %copy-done.45, s32[28]{0:T(128)S(1)} %copy-done.60, s32[28]{0:T(128)S(1)} %copy-done.59, bf16[1792,768]{1,0:T(8,128)(2,1)S(1)} %copy-done.11, ...), custom_call_target="tpu_custom_call" | custom-call | flops 11500000256 | tf_op jit(solution)/shard_map/ffn_back/pallas_call | solution.py:556
  225.3 2.1 fusion.refs_10_
  227.4 8.7 %collective-permute-start.25 = (bf16[2,3,192,512]{3,2,1,0:T(8,128)(2,1)S(1)}, bf16[2,3,192,512]{3,2,1,0:T(8,128)(2,1)S(1)}, u32[]{:S(2)}, u32[]{:S(2)}) collective-permute-start(bf16[2,3,192,512]{3,2,1,0:T(8,128)(2,1)S(1)} %fusion.refs_10_), channel_id=1, source_target_pairs={{0,16},{1,17},{2,18},{3,19},{4,20},{5,21},{6,22},{7,23},{8,24},{9,... | collective-permute-start | bytes 3538952 | tf_op jit(solution)/shard_map/ppermute | solution.py:1272
  236.1 21.9 %ffn_back.5 = (bf16[1792,1536]{1,0:T(8,128)(2,1)}, bf16[2,2,3,192,512]{4,3,2,1,0:T(8,128)(2,1)S(1)}, bf16[2,2,3,192,512]{4,3,2,1,0:T(8,128)(2,1)}) custom-call(s32[24]{0:T(128)S(1)} %copy-done.45, s32[28]{0:T(128)S(1)} %copy-done.60, s32[28]{0:T(128)S(1)} %copy-done.59, ...), custom_call_target="tpu_custom_call", output_to_operand_aliasing={{0}: (12, {})} | custom-call | flops 11500000256 | tf_op jit(solution)/shard_map/ffn_back/pallas_call | solution.py:556
  260.0 2.8 collective-permute-done.25
  265.5 2.1 fusion.1.refs_1_
  267.7 2.9 collective-permute-start.31
  270.6 2.6 copy-done.10
  275.6 8.8 %norm_one_back.1 = (f32[1792,768]{1,0:T(8,128)S(1)}, bf16[1792,768]{1,0:T(8,128)(2,1)S(1)}, f32[8,768]{1,0:T(8,128)S(1)}, bf16[2,2,96,768]{3,2,1,0:T(8,128)(2,1)S(1)}, bf16[2,2,96,768]{3,2,1,0:T(8,128)(2,1)S(1)}) custom-call(s32[24]{0:T(128)S(1)} %copy-done.46, bf16[1792,1536]{1,0:T(8,128)(2,1)S(1)} %copy-done.10, ...), custom_call_target="tpu_custom_call" | custom-call | flops 6000000000 | tf_op jit(solution)/shard_map/norm_one_back/pallas_call | solution.py:627
  284.4 2.4 copy-done.5
  286.8 2.6 fusion.10.refs_0_
  293.2 8.4 %attend_back.6.refs_0_ = bf16[1792,2304]{1,0:T(8,128)(2,1)} custom-call(s32[24]{0:T(128)S(1)} %copy-done.47, bf16[1792,2304]{1,0:T(8,128)(2,1)} %get-tuple-element.134.q_ref.k_ref.v_ref, bf16[1792,2304]{1,0:T(8,128)(2,1)} %get-tuple-element.134.q_ref.k_ref.v_ref, bf16[1792,2304]{1,0:T(8,128)(2,1)} %get-tuple-element.134.q_ref.k_ref.v_ref, ...), custom_call_target="tpu_custom_call" | custom-call | flops 5500000256 | tf_op jit(solution)/shard_map/attend_back/pallas_call | solution.py:747
  304.6 8.2 %attend_back.7.refs_0_ = bf16[1792,2304]{1,0:T(8,128)(2,1)} custom-call(s32[24]{0:T(128)S(1)} %copy-done.47, bf16[1792,2304]{1,0:T(8,128)(2,1)} %get-tuple-element.134.q_ref.k_ref.v_ref, bf16[1792,2304]{1,0:T(8,128)(2,1)} %get-tuple-element.134.q_ref.k_ref.v_ref, ...), custom_call_target="tpu_custom_call", output_to_operand_aliasing={{}: (9, {})} | custom-call | flops 5500000256 | tf_op jit(solution)/shard_map/attend_back/pallas_call | solution.py:747
  315.8 8.2 %attend_back.8.refs_0_ = bf16[1792,2304]{1,0:T(8,128)(2,1)} custom-call(s32[24]{0:T(128)S(1)} %copy-done.47, bf16[1792,2304]{1,0:T(8,128)(2,1)} %get-tuple-element.134.q_ref.k_ref.v_ref, bf16[1792,2304]{1,0:T(8,128)(2,1)} %get-tuple-element.134.q_ref.k_ref.v_ref, ...), custom_call_target="tpu_custom_call", output_to_operand_aliasing={{}: (9, {})} | custom-call | flops 5500000256 | tf_op jit(solution)/shard_map/attend_back/pallas_call | solution.py:747
  324.0 2.5 fusion.7.refs_2_
  326.5 5.9 %collective-permute-start.36 = (bf16[3,192,512]{2,1,0:T(8,128)(2,1)}, bf16[3,192,512]{2,1,0:T(8,128)(2,1)}, u32[]{:S(2)}, u32[]{:S(2)}) collective-permute-start(bf16[3,192,512]{2,1,0:T(8,128)(2,1)} %fusion.7.refs_2_), channel_id=1, source_target_pairs={{0,16},{1,17},{2,18},{3,19},{4,20},{5,21},{6,22},{7,23},{8,24},{9,... | collective-permute-start | bytes 1769480 | tf_op jit(solution)/shard_map/ppermute | solution.py:1272
  332.4 3.4 collective-permute-done.32
  335.9 8.4 %attend_back.9.refs_0_ = bf16[1792,2304]{1,0:T(8,128)(2,1)} custom-call(s32[24]{0:T(128)S(1)} %copy-done.47, bf16[1792,2304]{1,0:T(8,128)(2,1)} %get-tuple-element.134.q_ref.k_ref.v_ref, bf16[1792,2304]{1,0:T(8,128)(2,1)} %get-tuple-element.134.q_ref.k_ref.v_ref, ...), custom_call_target="tpu_custom_call", output_to_operand_aliasing={{}: (9, {})} | custom-call | flops 5500000256 | tf_op jit(solution)/shard_map/attend_back/pallas_call | solution.py:747
  344.3 2.5 fusion.6.refs_3_
  346.9 4.7 collective-permute-start.35
  351.6 8.3 %qkv_grad.2 = (bf16[2,2,96,2304]{3,2,1,0:T(8,128)(2,1)S(1)}, bf16[2,2,96,2304]{3,2,1,0:T(8,128)(2,1)}) custom-call(s32[24]{0:T(128)S(1)} %copy-done.47, bf16[1792,768]{1,0:T(8,128)(2,1)S(1)} %copy-done.19, bf16[1792,2304]{1,0:T(8,128)(2,1)} %attend_back.9.refs_0_, bf16[2,2,96,768]{3,2,1,0:T(8,128)(2,1)S(1)} %copy-done.65, ...), custom_call_target="tpu_custom_call" | custom-call | flops 4499999744 | tf_op jit(solution)/shard_map/qkv_grad/pallas_call | solution.py:802
  367.7 8.3 %attend_back.10.refs_0_ = bf16[1792,2304]{1,0:T(8,128)(2,1)} custom-call(s32[24]{0:T(128)S(1)} %copy-done.48, bf16[1792,2304]{1,0:T(8,128)(2,1)} %get-tuple-element.134.q_ref.k_ref.v_ref, bf16[1792,2304]{1,0:T(8,128)(2,1)} %get-tuple-element.134.q_ref.k_ref.v_ref, ...), custom_call_target="tpu_custom_call", output_to_operand_aliasing={{}: (9, {})} | custom-call | flops 5500000256 | tf_op jit(solution)/shard_map/attend_back/pallas_call | solution.py:747
  376.0 2.3 collective-permute-done.38
  380.6 2.3 fusion.12.refs_3_
  382.9 8.2 %attend_back.11.refs_0_.refs_2_.refs_3_ = bf16[1792,2304]{1,0:T(8,128)(2,1)} custom-call(s32[24]{0:T(128)S(1)} %copy-done.48, bf16[1792,2304]{1,0:T(8,128)(2,1)} %get-tuple-element.134.q_ref.k_ref.v_ref, bf16[1792,2304]{1,0:T(8,128)(2,1)} %get-tuple-element.134.q_ref.k_ref.v_ref, ...), custom_call_target="tpu_custom_call", output_to_operand_aliasing={{}: (9, {})} | custom-call | flops 5500000256 | tf_op jit(solution)/shard_map/attend_back/pallas_call | solution.py:747
  392.5 7.3 %collective-permute-done.42 = bf16[3,192,512]{2,1,0:T(8,128)(2,1)S(1)} collective-permute-done((bf16[3,192,512]{2,1,0:T(8,128)(2,1)S(1)}, bf16[3,192,512]{2,1,0:T(8,128)(2,1)S(1)}, u32[]{:S(2)}, u32[]{:S(2)}) %collective-permute-start.42) | collective-permute-done | bytes 589856 | tf_op jit(solution)/shard_map/ppermute | solution.py:1298
  402.5 2.9 wide_unfold.2
  405.9 2.5 copy-done.6
  408.4 5.6 %qkv_grad.3 = (bf16[2,2,96,768]{3,2,1,0:T(8,128)(2,1)S(1)}, bf16[2,2,96,768]{3,2,1,0:T(8,128)(2,1)S(1)}) custom-call(s32[24]{0:T(128)S(1)} %copy-done.49, bf16[1792,768]{1,0:T(8,128)(2,1)S(1)} %copy-done.20, bf16[1792,2304]{1,0:T(8,128)(2,1)} %attend_back.11.refs_0_.refs_2_.refs_3_, bf16[3,192,512]{2,1,0:T(8,128)(2,1)S(1)} %copy-done.23, ...), custom_call_target="tpu_custom_call" | custom-call | flops 4499999744 | tf_op jit(solution)/shard_map/qkv_grad/pallas_call | solution.py:802
  415.6 3.6 collective-permute-start.44
  419.8 7.0 %token_grad.2.refs_5_.refs_0_ = f32[2,768,768]{2,1,0:T(8,128)} custom-call(s32[24]{0:T(128)S(1)} %copy-done.49, f32[1792,768]{1,0:T(8,128)} %copy-done.5, f32[1792,768]{1,0:T(8,128)} %copy-done.5, bf16[1792,2304]{1,0:T(8,128)(2,1)} %attend_back.11.refs_0_.refs_2_.refs_3_, bf16[1792,2304]{1,0:T(8,128)(2,1)} %attend_back.11.refs_0_.refs_2_.refs_3_, ...), custom_call_target="tpu_custom_call" | custom-call | flops 4499999744 | tf_op jit(solution)/shard_map/token_grad/pallas_call | solution.py:882
  426.8 2.2 collective-permute-done.44
  430.4 2.3 collective-permute-start.49
  434.6 2.3 copy-done.8
  437.0 7.8 %token_grad.3 = (bf16[768,768]{1,0:T(8,128)(2,1)S(1)}, f32[2,64,768]{2,1,0:T(8,128)}) custom-call(s32[24]{0:T(128)S(1)} %copy-done.49, f32[1792,768]{1,0:T(8,128)} %copy-done.5, f32[1792,768]{1,0:T(8,128)} %copy-done.5, bf16[1792,2304]{1,0:T(8,128)(2,1)} %attend_back.11.refs_0_.refs_2_.refs_3_, bf16[1792,2304]{1,0:T(8,128)(2,1)} %attend_back.11.refs_0_.refs_2_.refs_3_, ...), custom_call_target="tpu_custom_call" | custom-call | flops 4499999744 | tf_op jit(solution)/shard_map/token_grad/pallas_call | solution.py:882
  446.4 3.1 collective-permute-done.51
  454.0 2.6 wide_unfold.3
  459.1 2.3 copy-done.7
  461.5 3.9 place_moved.1.refs_3_
  465.4 5.1 %collective-permute-done.55 = bf16[96,2304]{1,0:T(8,128)(2,1)S(1)} collective-permute-done((bf16[96,2304]{1,0:T(8,128)(2,1)S(1)}, bf16[96,2304]{1,0:T(8,128)(2,1)S(1)}, u32[]{:S(2)}, u32[]{:S(2)}) %collective-permute-start.55) | collective-permute-done | bytes 442400 | tf_op jit(solution)/shard_map/ppermute | solution.py:1298
  473.5 2.3 collective-permute-done.56
  477.3 4.5 collective-permute-start.62
  483.0 2.1 collective-permute-done.62
  487.1 2.3 copy-done.9
  489.4 3.3 wide_unfold_parts.1
  492.8 6.7 %all_gather.15 = bf16[384,768]{1,0:T(8,128)(2,1)S(1)} all-gather(bf16[96,768]{1,0:T(8,128)(2,1)S(1)} %broadcast_select_fusion.4), channel_id=1, replica_groups={{0,1,2,3},{4,5,6,7},{8,9,10,11},{12,13,14,15},{16,17,18,19},{20,21,22,2..., dimensions={0}, use_global_device_ids=true | all-gather | bytes 737280 | tf_op jit(solution)/shard_map/all_gather | solution.py:1349
  (345 shorter events, 96.0 us)
Async XLA Ops:
  7.2 393.7 %all-gather.4.cloned.1.call-start = ((), (), s32[]{:S(2)}) async-start(), calls=%async_computation | async-start | bytes 2949120 | tf_op jit(solution)/shard_map/all_gather | solution.py:1349
  16.2 3.1 collective-permute-start.1
  16.6 23.1 %collective-permute-start.2 = (bf16[192,2304]{1,0:T(8,128)(2,1)}, bf16[192,2304]{1,0:T(8,128)(2,1)}, u32[]{:S(2)}, u32[]{:S(2)}) collective-permute-start(bf16[192,2304]{1,0:T(8,128)(2,1)} %constant_dynamic-slice_fusion.4), channel_id=1, source_target_pairs={{0,16},{1,17},{2,18},{3,19},{4,20},{5,21},{6,22},{7,23},{8,24},{9,... | collective-permute-start | bytes 2654216 | tf_op jit(solution)/shard_map/ppermute | solution.py:1272
  39.7 6.0 %collective-permute-start.3 = (bf16[192,2304]{1,0:T(8,128)(2,1)}, bf16[192,2304]{1,0:T(8,128)(2,1)}, u32[]{:S(2)}, u32[]{:S(2)}) collective-permute-start(bf16[192,2304]{1,0:T(8,128)(2,1)} %collective-permute-done.2.refs_1_), channel_id=1, source_target_pairs={{0,1},{1,0},{2,3},{3,2},{4,5},{5,4},{6,7},{7,6},{8,9},{9,8},{10,11... | collective-permute-start | bytes 2654216 | tf_op jit(solution)/shard_map/ppermute | solution.py:1272
  43.6 29.9 %collective-permute-start.5 = (bf16[192,768]{1,0:T(8,128)(2,1)S(1)}, bf16[192,768]{1,0:T(8,128)(2,1)S(1)}, u32[]{:S(2)}, u32[]{:S(2)}) collective-permute-start(bf16[192,768]{1,0:T(8,128)(2,1)S(1)} %constant_dynamic-slice_fusion.3.refs_3_), channel_id=1, source_target_pairs={{0,16},{1,17},{2,18},{3,19},{4,20},{5,21},{6,22},{7,23},{8,24},{9,... | collective-permute-start | bytes 884744 | tf_op jit(solution)/shard_map/ppermute | solution.py:1272
  45.4 28.1 %collective-permute-start.6 = (bf16[96,3072]{1,0:T(8,128)(2,1)S(1)}, bf16[96,3072]{1,0:T(8,128)(2,1)S(1)}, u32[]{:S(2)}, u32[]{:S(2)}) collective-permute-start(bf16[96,3072]{1,0:T(8,128)(2,1)S(1)} %constant_dynamic-slice_fusion.2.refs_4_), channel_id=1, source_target_pairs={{0,16},{1,17},{2,18},{3,19},{4,20},{5,21},{6,22},{7,23},{8,24},{9,... | collective-permute-start | bytes 1769480 | tf_op jit(solution)/shard_map/ppermute | solution.py:1272
  56.6 26.1 %collective-permute-start.9 = (bf16[96,3072]{1,0:T(8,128)(2,1)S(1)}, bf16[96,3072]{1,0:T(8,128)(2,1)S(1)}, u32[]{:S(2)}, u32[]{:S(2)}) collective-permute-start(bf16[96,3072]{1,0:T(8,128)(2,1)S(1)} %constant_dynamic-slice_fusion.1.refs_0_), channel_id=1, source_target_pairs={{0,16},{1,17},{2,18},{3,19},{4,20},{5,21},{6,22},{7,23},{8,24},{9,... | collective-permute-start | bytes 1769480 | tf_op jit(solution)/shard_map/ppermute | solution.py:1272
  70.3 12.3 %collective-permute-start.4 = (bf16[4,384]{1,0:T(4,128)(2,1)S(1)}, bf16[4,384]{1,0:T(4,128)(2,1)S(1)}, u32[]{:S(2)}, u32[]{:S(2)}) collective-permute-start(bf16[4,384]{1,0:T(4,128)(2,1)S(1)} %pad_maximum_fusion), channel_id=1, source_target_pairs={{0,16},{1,17},{2,18},{3,19},{4,20},{5,21},{6,22},{7,23},{8,24},{9,... | collective-permute-start | bytes 9224 | tf_op jit(solution)/shard_map/ppermute | solution.py:1272
  73.4 17.0 %collective-permute-start.7 = (bf16[192,768]{1,0:T(8,128)(2,1)S(1)}, bf16[192,768]{1,0:T(8,128)(2,1)S(1)}, u32[]{:S(2)}, u32[]{:S(2)}) collective-permute-start(bf16[192,768]{1,0:T(8,128)(2,1)S(1)} %collective-permute-done.5.refs_2_.refs_1_), channel_id=1, source_target_pairs={{0,1},{1,0},{2,3},{3,2},{4,5},{5,4},{6,7},{7,6},{8,9},{9,8},{10,11... | collective-permute-start | bytes 884744 | tf_op jit(solution)/shard_map/ppermute | solution.py:1272
  74.9 15.3 %collective-permute-start.8 = (bf16[96,3072]{1,0:T(8,128)(2,1)S(1)}, bf16[96,3072]{1,0:T(8,128)(2,1)S(1)}, u32[]{:S(2)}, u32[]{:S(2)}) collective-permute-start(bf16[96,3072]{1,0:T(8,128)(2,1)S(1)} %collective-permute-done.6.refs_3_.refs_4_), channel_id=1, source_target_pairs={{0,2},{1,3},{2,0},{3,1},{4,6},{5,7},{6,4},{7,5},{8,10},{9,11},{10,... | collective-permute-start | bytes 1769480 | tf_op jit(solution)/shard_map/ppermute | solution.py:1272
  74.9 29.8 %collective-permute-start.13 = (bf16[768,768]{1,0:T(8,128)(2,1)S(1)}, bf16[768,768]{1,0:T(8,128)(2,1)S(1)}, u32[]{:S(2)}, u32[]{:S(2)}) collective-permute-start(bf16[768,768]{1,0:T(8,128)(2,1)S(1)} %constant_dynamic-slice_fusion.refs_4_), channel_id=1, source_target_pairs={{0,16},{1,17},{2,18},{3,19},{4,20},{5,21},{6,22},{7,23},{8,24},{9,... | collective-permute-start | bytes 3538952 | tf_op jit(solution)/shard_map/ppermute | solution.py:1272
  90.2 14.5 %collective-permute-start.12 = (bf16[96,3072]{1,0:T(8,128)(2,1)S(1)}, bf16[96,3072]{1,0:T(8,128)(2,1)S(1)}, u32[]{:S(2)}, u32[]{:S(2)}) collective-permute-start(bf16[96,3072]{1,0:T(8,128)(2,1)S(1)} %collective-permute-done.9.refs_4_.refs_9_), channel_id=1, source_target_pairs={{0,2},{1,3},{2,0},{3,1},{4,6},{5,7},{6,4},{7,5},{8,10},{9,11},{10,... | collective-permute-start | bytes 1769480 | tf_op jit(solution)/shard_map/ppermute | solution.py:1272
  104.7 6.3 %collective-permute-start.16 = (bf16[768,768]{1,0:T(8,128)(2,1)S(1)}, bf16[768,768]{1,0:T(8,128)(2,1)S(1)}, u32[]{:S(2)}, u32[]{:S(2)}) collective-permute-start(bf16[768,768]{1,0:T(8,128)(2,1)S(1)} %collective-permute-done.13.refs_14_), channel_id=1, source_target_pairs={{0,1},{1,0},{2,3},{3,2},{4,5},{5,4},{6,7},{7,6},{8,9},{9,8},{10,11... | collective-permute-start | bytes 3538952 | tf_op jit(solution)/shard_map/ppermute | solution.py:1272
  104.7 3.7 collective-permute-start.10
  105.2 4.0 collective-permute-start.11
  105.3 4.8 collective-permute-start.14
  105.8 5.2 %collective-permute-start.15 = (bf16[96,3072]{1,0:T(8,128)(2,1)S(1)}, bf16[96,3072]{1,0:T(8,128)(2,1)S(1)}, u32[]{:S(2)}, u32[]{:S(2)}) collective-permute-start(bf16[96,3072]{1,0:T(8,128)(2,1)S(1)} %collective-permute-done.12.refs_10_), channel_id=1, source_target_pairs={{0,1},{1,0},{2,3},{3,2},{4,5},{5,4},{6,7},{7,6},{8,9},{9,8},{10,11... | collective-permute-start | bytes 1769480 | tf_op jit(solution)/shard_map/ppermute | solution.py:1272
  153.5 12.0 %collective-permute-start.18 = (bf16[16,512]{1,0:T(8,128)(2,1)S(1)}, bf16[16,512]{1,0:T(8,128)(2,1)S(1)}, u32[]{:S(2)}, u32[]{:S(2)}) collective-permute-start(bf16[16,512]{1,0:T(8,128)(2,1)S(1)} %get-tuple-element.252), channel_id=1, source_target_pairs={{0,16},{1,17},{2,18},{3,19},{4,20},{5,21},{6,22},{7,23},{8,24},{9,... | collective-permute-start | bytes 49160 | tf_op jit(solution)/shard_map/ppermute | solution.py:1272
  163.8 4.6 collective-permute-start.20
  163.8 3.9 collective-permute-start.19
  168.4 4.3 collective-permute-start.23
  168.4 5.7 %collective-permute-start.22 = (bf16[64,512]{1,0:T(8,128)(2,1)S(1)}, bf16[64,512]{1,0:T(8,128)(2,1)S(1)}, u32[]{:S(2)}, u32[]{:S(2)}) collective-permute-start(bf16[64,512]{1,0:T(8,128)(2,1)S(1)} %constant_dynamic-update-slice_fusion.2.refs_0_), channel_id=1, source_target_pairs={{0,8},{1,9},{2,10},{3,11},{4,12},{5,13},{6,14},{7,15},{8,0},{9,1},... | collective-permute-start | bytes 196616 | tf_op jit(solution)/shard_map/ppermute | solution.py:1289
  168.4 7.3 %collective-permute-start.21 = (bf16[64,512]{1,0:T(8,128)(2,1)S(1)}, bf16[64,512]{1,0:T(8,128)(2,1)S(1)}, u32[]{:S(2)}, u32[]{:S(2)}) collective-permute-start(bf16[64,512]{1,0:T(8,128)(2,1)S(1)} %constant_dynamic-update-slice_fusion.2.refs_0_), channel_id=1, source_target_pairs={{0,4},{1,5},{2,6},{3,7},{4,8},{5,9},{6,10},{7,11},{8,12},{9,13},{1... | collective-permute-start | bytes 196616 | tf_op jit(solution)/shard_map/ppermute | solution.py:1289
  203.6 21.7 %collective-permute-start.24 = (bf16[2,2,3,192,512]{4,3,2,1,0:T(8,128)(2,1)S(1)}, bf16[2,2,3,192,512]{4,3,2,1,0:T(8,128)(2,1)}, u32[]{:S(2)}, u32[]{:S(2)}) collective-permute-start(bf16[2,2,3,192,512]{4,3,2,1,0:T(8,128)(2,1)S(1)} %get-tuple-element.172.refs_9_), channel_id=1, source_target_pairs={{0,1},{1,0},{2,3},{3,2},{4,5},{5,4},{6,7},{7,6},{8,9},{9,8},{10,11... | collective-permute-start | bytes 7077896 | tf_op jit(solution)/shard_map/ppermute | solution.py:1272
  224.9 35.1 %collective-permute-start.26 = (bf16[2,2,3,192,512]{4,3,2,1,0:T(8,128)(2,1)}, bf16[2,2,3,192,512]{4,3,2,1,0:T(8,128)(2,1)}, u32[]{:S(2)}, u32[]{:S(2)}) collective-permute-start(bf16[2,2,3,192,512]{4,3,2,1,0:T(8,128)(2,1)} %get-tuple-element.177.refs_11_), channel_id=1, source_target_pairs={{0,1},{1,0},{2,3},{3,2},{4,5},{5,4},{6,7},{7,6},{8,9},{9,8},{10,11... | collective-permute-start | bytes 7077896 | tf_op jit(solution)/shard_map/ppermute | solution.py:1272
  227.4 35.4 %collective-permute-start.25 = (bf16[2,3,192,512]{3,2,1,0:T(8,128)(2,1)S(1)}, bf16[2,3,192,512]{3,2,1,0:T(8,128)(2,1)S(1)}, u32[]{:S(2)}, u32[]{:S(2)}) collective-permute-start(bf16[2,3,192,512]{3,2,1,0:T(8,128)(2,1)S(1)} %fusion.refs_10_), channel_id=1, source_target_pairs={{0,16},{1,17},{2,18},{3,19},{4,20},{5,21},{6,22},{7,23},{8,24},{9,... | collective-permute-start | bytes 3538952 | tf_op jit(solution)/shard_map/ppermute | solution.py:1272
  259.4 31.5 %collective-permute-start.28 = (bf16[2,2,3,192,512]{4,3,2,1,0:T(8,128)(2,1)}, bf16[2,2,3,192,512]{4,3,2,1,0:T(8,128)(2,1)}, u32[]{:S(2)}, u32[]{:S(2)}) collective-permute-start(bf16[2,2,3,192,512]{4,3,2,1,0:T(8,128)(2,1)} %get-tuple-element.187.refs_2_), channel_id=1, source_target_pairs={{0,1},{1,0},{2,3},{3,2},{4,5},{5,4},{6,7},{7,6},{8,9},{9,8},{10,11... | collective-permute-start | bytes 7077896 | tf_op jit(solution)/shard_map/ppermute | solution.py:1272
  265.4 21.3 %collective-permute-start.27 = (bf16[3,192,512]{2,1,0:T(8,128)(2,1)S(1)}, bf16[3,192,512]{2,1,0:T(8,128)(2,1)S(1)}, u32[]{:S(2)}, u32[]{:S(2)}) collective-permute-start(bf16[3,192,512]{2,1,0:T(8,128)(2,1)S(1)} %fusion.11.refs_0_), channel_id=1, source_target_pairs={{0,2},{1,3},{2,0},{3,1},{4,6},{5,7},{6,4},{7,5},{8,10},{9,11},{10,... | collective-permute-start | bytes 1769480 | tf_op jit(solution)/shard_map/ppermute | solution.py:1272
  267.7 45.1 %collective-permute-start.31 = (bf16[2,3,192,512]{3,2,1,0:T(8,128)(2,1)S(1)}, bf16[2,3,192,512]{3,2,1,0:T(8,128)(2,1)}, u32[]{:S(2)}, u32[]{:S(2)}) collective-permute-start(bf16[2,3,192,512]{3,2,1,0:T(8,128)(2,1)S(1)} %fusion.1.refs_1_), channel_id=1, source_target_pairs={{0,16},{1,17},{2,18},{3,19},{4,20},{5,21},{6,22},{7,23},{8,24},{9,... | collective-permute-start | bytes 3538952 | tf_op jit(solution)/shard_map/ppermute | solution.py:1272
  289.4 14.2 %collective-permute-start.29 = (bf16[3,192,512]{2,1,0:T(8,128)(2,1)S(1)}, bf16[3,192,512]{2,1,0:T(8,128)(2,1)S(1)}, u32[]{:S(2)}, u32[]{:S(2)}) collective-permute-start(bf16[3,192,512]{2,1,0:T(8,128)(2,1)S(1)} %fusion.10.refs_0_), channel_id=1, source_target_pairs={{0,4},{1,5},{2,6},{3,7},{12,8},{13,9},{14,10},{15,11},{16,20},{17,... | collective-permute-start | bytes 1769480 | tf_op jit(solution)/shard_map/ppermute | solution.py:1298
  292.6 31.4 %collective-permute-start.33 = (bf16[2,3,192,512]{3,2,1,0:T(8,128)(2,1)S(1)}, bf16[2,3,192,512]{3,2,1,0:T(8,128)(2,1)S(1)}, u32[]{:S(2)}, u32[]{:S(2)}) collective-permute-start(bf16[2,3,192,512]{3,2,1,0:T(8,128)(2,1)S(1)} %fusion.2.refs_1_), channel_id=1, source_target_pairs={{0,2},{1,3},{2,0},{3,1},{4,6},{5,7},{6,4},{7,5},{8,10},{9,11},{10,... | collective-permute-start | bytes 3538952 | tf_op jit(solution)/shard_map/ppermute | solution.py:1272
  303.8 10.6 %collective-permute-start.30 = (bf16[3,192,512]{2,1,0:T(8,128)(2,1)S(1)}, bf16[3,192,512]{2,1,0:T(8,128)(2,1)S(1)}, u32[]{:S(2)}, u32[]{:S(2)}) collective-permute-start(bf16[3,192,512]{2,1,0:T(8,128)(2,1)S(1)} %add_convert_fusion.9.refs_1_), channel_id=1, source_target_pairs={{4,8},{5,9},{6,10},{7,11},{8,4},{9,5},{10,6},{11,7},{20,24},{21,25... | collective-permute-start | bytes 1769480 | tf_op jit(solution)/shard_map/ppermute | solution.py:1298
  314.2 30.1 %collective-permute-start.34 = (bf16[3,192,512]{2,1,0:T(8,128)(2,1)S(1)}, bf16[3,192,512]{2,1,0:T(8,128)(2,1)S(1)}, u32[]{:S(2)}, u32[]{:S(2)}) collective-permute-start(bf16[3,192,512]{2,1,0:T(8,128)(2,1)S(1)} %fusion.8.refs_2_), channel_id=1, source_target_pairs={{0,2},{1,3},{2,0},{3,1},{4,6},{5,7},{6,4},{7,5},{8,10},{9,11},{10,... | collective-permute-start | bytes 1769480 | tf_op jit(solution)/shard_map/ppermute | solution.py:1272
  314.5 21.3 %collective-permute-start.32 = (bf16[3,192,512]{2,1,0:T(8,128)(2,1)S(1)}, bf16[3,192,512]{2,1,0:T(8,128)(2,1)S(1)}, u32[]{:S(2)}, u32[]{:S(2)}) collective-permute-start(bf16[3,192,512]{2,1,0:T(8,128)(2,1)S(1)} %add_convert_fusion.8.refs_1_), channel_id=1, source_target_pairs={{4,0},{5,1},{6,2},{7,3},{8,12},{9,13},{10,14},{11,15},{20,16},{21,... | collective-permute-start | bytes 1769480 | tf_op jit(solution)/shard_map/ppermute | solution.py:1298
  326.5 35.2 %collective-permute-start.36 = (bf16[3,192,512]{2,1,0:T(8,128)(2,1)}, bf16[3,192,512]{2,1,0:T(8,128)(2,1)}, u32[]{:S(2)}, u32[]{:S(2)}) collective-permute-start(bf16[3,192,512]{2,1,0:T(8,128)(2,1)} %fusion.7.refs_2_), channel_id=1, source_target_pairs={{0,16},{1,17},{2,18},{3,19},{4,20},{5,21},{6,22},{7,23},{8,24},{9,... | collective-permute-start | bytes 1769480 | tf_op jit(solution)/shard_map/ppermute | solution.py:1272
  346.9 18.7 %collective-permute-start.35 = (bf16[3,192,512]{2,1,0:T(8,128)(2,1)}, bf16[3,192,512]{2,1,0:T(8,128)(2,1)}, u32[]{:S(2)}, u32[]{:S(2)}) collective-permute-start(bf16[3,192,512]{2,1,0:T(8,128)(2,1)} %fusion.6.refs_3_), channel_id=1, source_target_pairs={{0,4},{1,5},{2,6},{3,7},{12,8},{13,9},{14,10},{15,11},{16,20},{17,... | collective-permute-start | bytes 1769480 | tf_op jit(solution)/shard_map/ppermute | solution.py:1298
  361.1 19.5 %collective-permute-start.39 = (bf16[2,2,96,2304]{3,2,1,0:T(8,128)(2,1)}, bf16[2,2,96,2304]{3,2,1,0:T(8,128)(2,1)}, u32[]{:S(2)}, u32[]{:S(2)}) collective-permute-start(bf16[2,2,96,2304]{3,2,1,0:T(8,128)(2,1)} %get-tuple-element.205.refs_3_), channel_id=1, source_target_pairs={{0,1},{1,0},{2,3},{3,2},{4,5},{5,4},{6,7},{7,6},{8,9},{9,8},{10,11... | collective-permute-start | bytes 5308424 | tf_op jit(solution)/shard_map/ppermute | solution.py:1272
  361.7 90.6 %all-gather.6.cloned.1.call-start = ((), (), s32[]{:S(2)}) async-start(), calls=%async_computation.1 | async-start | bytes 2949120 | tf_op jit(solution)/shard_map/all_gather | solution.py:1349
  363.8 14.4 %collective-permute-start.38 = (bf16[3,192,512]{2,1,0:T(8,128)(2,1)S(1)}, bf16[3,192,512]{2,1,0:T(8,128)(2,1)S(1)}, u32[]{:S(2)}, u32[]{:S(2)}) collective-permute-start(bf16[3,192,512]{2,1,0:T(8,128)(2,1)S(1)} %fusion.4.refs_2_), channel_id=1, source_target_pairs={{0,4},{1,5},{2,6},{3,7},{12,8},{13,9},{14,10},{15,11},{16,20},{17,... | collective-permute-start | bytes 1769480 | tf_op jit(solution)/shard_map/ppermute | solution.py:1298
  367.0 12.2 %collective-permute-start.37 = (bf16[3,192,512]{2,1,0:T(8,128)(2,1)S(1)}, bf16[3,192,512]{2,1,0:T(8,128)(2,1)S(1)}, u32[]{:S(2)}, u32[]{:S(2)}) collective-permute-start(bf16[3,192,512]{2,1,0:T(8,128)(2,1)S(1)} %add_convert_fusion.7.refs_1_), channel_id=1, source_target_pairs={{4,8},{5,9},{6,10},{7,11},{8,4},{9,5},{10,6},{11,7},{20,24},{21,25... | collective-permute-start | bytes 1769480 | tf_op jit(solution)/shard_map/ppermute | solution.py:1298
  378.4 12.7 %collective-permute-start.40 = (bf16[3,192,512]{2,1,0:T(8,128)(2,1)S(1)}, bf16[3,192,512]{2,1,0:T(8,128)(2,1)S(1)}, u32[]{:S(2)}, u32[]{:S(2)}) collective-permute-start(bf16[3,192,512]{2,1,0:T(8,128)(2,1)S(1)} %add_convert_fusion.5.refs_2_), channel_id=1, source_target_pairs={{4,8},{5,9},{6,10},{7,11},{8,4},{9,5},{10,6},{11,7},{20,24},{21,25... | collective-permute-start | bytes 1769480 | tf_op jit(solution)/shard_map/ppermute | solution.py:1298
  379.3 20.6 %collective-permute-start.42 = (bf16[3,192,512]{2,1,0:T(8,128)(2,1)S(1)}, bf16[3,192,512]{2,1,0:T(8,128)(2,1)S(1)}, u32[]{:S(2)}, u32[]{:S(2)}) collective-permute-start(bf16[3,192,512]{2,1,0:T(8,128)(2,1)S(1)} %add_convert_fusion.6.refs_1_), channel_id=1, source_target_pairs={{4,0},{5,1},{6,2},{7,3},{8,12},{9,13},{10,14},{11,15},{20,16},{21,... | collective-permute-start | bytes 1769480 | tf_op jit(solution)/shard_map/ppermute | solution.py:1298
  382.9 31.2 %collective-permute-start.43 = (bf16[2,96,2304]{2,1,0:T(8,128)(2,1)}, bf16[2,96,2304]{2,1,0:T(8,128)(2,1)}, u32[]{:S(2)}, u32[]{:S(2)}) collective-permute-start(bf16[2,96,2304]{2,1,0:T(8,128)(2,1)} %fusion.12.refs_3_), channel_id=1, source_target_pairs={{0,2},{1,3},{2,0},{3,1},{4,6},{5,7},{6,4},{7,5},{8,10},{9,11},{10,... | collective-permute-start | bytes 2654216 | tf_op jit(solution)/shard_map/ppermute | solution.py:1272
  391.2 22.8 %collective-permute-start.41 = (bf16[3,192,512]{2,1,0:T(8,128)(2,1)S(1)}, bf16[3,192,512]{2,1,0:T(8,128)(2,1)S(1)}, u32[]{:S(2)}, u32[]{:S(2)}) collective-permute-start(bf16[3,192,512]{2,1,0:T(8,128)(2,1)S(1)} %add_convert_fusion.4.refs_2_), channel_id=1, source_target_pairs={{4,0},{5,1},{6,2},{7,3},{8,12},{9,13},{10,14},{11,15},{20,16},{21,... | collective-permute-start | bytes 1769480 | tf_op jit(solution)/shard_map/ppermute | solution.py:1298
  400.8 98.7 %all-gather.8.cloned.1.call-start = ((), (), s32[]{:S(2)}) async-start(), calls=%async_computation.2 | async-start | bytes 2211840 | tf_op jit(solution)/shard_map/all_gather | solution.py:1349
  415.6 13.4 %collective-permute-start.44 = (bf16[96,2304]{1,0:T(8,128)(2,1)S(1)}, bf16[96,2304]{1,0:T(8,128)(2,1)S(1)}, u32[]{:S(2)}, u32[]{:S(2)}) collective-permute-start(bf16[96,2304]{1,0:T(8,128)(2,1)S(1)} %fusion.15.refs_6_), channel_id=1, source_target_pairs={{0,16},{1,17},{2,18},{3,19},{4,20},{5,21},{6,22},{7,23},{8,24},{9,... | collective-permute-start | bytes 1327112 | tf_op jit(solution)/shard_map/ppermute | solution.py:1272
  419.3 7.6 %collective-permute-start.46 = (f32[8,768]{1,0:T(8,128)S(1)}, f32[8,768]{1,0:T(8,128)S(1)}, u32[]{:S(2)}, u32[]{:S(2)}) collective-permute-start(f32[8,768]{1,0:T(8,128)S(1)} %copy-done.54), channel_id=1, source_target_pairs={{0,1},{1,0},{2,3},{3,2},{4,5},{5,4},{6,7},{7,6},{8,9},{9,8},{10,11... | collective-permute-start | bytes 73736 | tf_op jit(solution)/shard_map/ppermute | solution.py:1272
  419.3 30.1 %collective-permute-start.48 = (bf16[3,192,512]{2,1,0:T(8,128)(2,1)S(1)}, bf16[3,192,512]{2,1,0:T(8,128)(2,1)S(1)}, u32[]{:S(2)}, u32[]{:S(2)}) collective-permute-start(bf16[3,192,512]{2,1,0:T(8,128)(2,1)S(1)} %broadcast_select_fusion.refs_5_.p00), channel_id=1, source_target_pairs={{0,2},{1,3},{2,0},{3,1},{4,6},{5,7},{6,4},{7,5},{8,10},{9,11},{10,... | collective-permute-start | bytes 1769480 | tf_op jit(solution)/shard_map/ppermute | solution.py:1272
  419.4 13.3 %collective-permute-start.45 = (bf16[2,2,96,768]{3,2,1,0:T(8,128)(2,1)S(1)}, bf16[2,2,96,768]{3,2,1,0:T(8,128)(2,1)S(1)}, u32[]{:S(2)}, u32[]{:S(2)}) collective-permute-start(bf16[2,2,96,768]{3,2,1,0:T(8,128)(2,1)S(1)} %get-tuple-element.217.refs_7_), channel_id=1, source_target_pairs={{0,1},{1,0},{2,3},{3,2},{4,5},{5,4},{6,7},{7,6},{8,9},{9,8},{10,11... | collective-permute-start | bytes 1769480 | tf_op jit(solution)/shard_map/ppermute | solution.py:1272
  430.4 14.3 %collective-permute-start.49 = (bf16[96,2304]{1,0:T(8,128)(2,1)S(1)}, bf16[96,2304]{1,0:T(8,128)(2,1)S(1)}, u32[]{:S(2)}, u32[]{:S(2)}) collective-permute-start(bf16[96,2304]{1,0:T(8,128)(2,1)S(1)} %fusion.14.refs_6_), channel_id=1, source_target_pairs={{0,4},{1,5},{2,6},{3,7},{12,8},{13,9},{14,10},{15,11},{16,20},{17,... | collective-permute-start | bytes 1327112 | tf_op jit(solution)/shard_map/ppermute | solution.py:1298
  432.8 16.7 %collective-permute-start.50 = (bf16[2,96,768]{2,1,0:T(8,128)(2,1)S(1)}, bf16[2,96,768]{2,1,0:T(8,128)(2,1)S(1)}, u32[]{:S(2)}, u32[]{:S(2)}) collective-permute-start(bf16[2,96,768]{2,1,0:T(8,128)(2,1)S(1)} %fusion.16.refs_7_), channel_id=1, source_target_pairs={{0,16},{1,17},{2,18},{3,19},{4,20},{5,21},{6,22},{7,23},{8,24},{9,... | collective-permute-start | bytes 884744 | tf_op jit(solution)/shard_map/ppermute | solution.py:1272
  444.9 11.7 %collective-permute-start.52 = (bf16[96,2304]{1,0:T(8,128)(2,1)S(1)}, bf16[96,2304]{1,0:T(8,128)(2,1)S(1)}, u32[]{:S(2)}, u32[]{:S(2)}) collective-permute-start(bf16[96,2304]{1,0:T(8,128)(2,1)S(1)} %add_convert_fusion.11.refs_4_), channel_id=1, source_target_pairs={{4,8},{5,9},{6,10},{7,11},{8,4},{9,5},{10,6},{11,7},{20,24},{21,25... | collective-permute-start | bytes 1327112 | tf_op jit(solution)/shard_map/ppermute | solution.py:1298
  445.6 3.9 collective-permute-start.51
  449.5 9.7 %collective-permute-start.47 = (bf16[768,768]{1,0:T(8,128)(2,1)S(1)}, bf16[768,768]{1,0:T(8,128)(2,1)}, u32[]{:S(2)}, u32[]{:S(2)}) collective-permute-start(bf16[768,768]{1,0:T(8,128)(2,1)S(1)} %get-tuple-element.223.own_ref), channel_id=1, source_target_pairs={{0,1},{1,0},{2,3},{3,2},{4,5},{5,4},{6,7},{7,6},{8,9},{9,8},{10,11... | collective-permute-start | bytes 3538952 | tf_op jit(solution)/shard_map/ppermute | solution.py:1272
  449.5 8.5 %collective-permute-start.54 = (f32[8,768]{1,0:T(8,128)S(1)}, f32[8,768]{1,0:T(8,128)S(1)}, u32[]{:S(2)}, u32[]{:S(2)}) collective-permute-start(f32[8,768]{1,0:T(8,128)S(1)} %add.255.refs_6_), channel_id=1, source_target_pairs={{0,2},{1,3},{2,0},{3,1},{4,6},{5,7},{6,4},{7,5},{8,10},{9,11},{10,... | collective-permute-start | bytes 73736 | tf_op jit(solution)/shard_map/ppermute | solution.py:1272
  450.3 7.7 %collective-permute-start.53 = (bf16[96,768]{1,0:T(8,128)(2,1)S(1)}, bf16[96,768]{1,0:T(8,128)(2,1)}, u32[]{:S(2)}, u32[]{:S(2)}) collective-permute-start(bf16[96,768]{1,0:T(8,128)(2,1)S(1)} %fusion.19.refs_5_), channel_id=1, source_target_pairs={{0,2},{1,3},{2,0},{3,1},{4,6},{5,7},{6,4},{7,5},{8,10},{9,11},{10,... | collective-permute-start | bytes 442376 | tf_op jit(solution)/shard_map/ppermute | solution.py:1272
  456.6 13.9 %collective-permute-start.55 = (bf16[96,2304]{1,0:T(8,128)(2,1)S(1)}, bf16[96,2304]{1,0:T(8,128)(2,1)S(1)}, u32[]{:S(2)}, u32[]{:S(2)}) collective-permute-start(bf16[96,2304]{1,0:T(8,128)(2,1)S(1)} %add_convert_fusion.10.refs_2_), channel_id=1, source_target_pairs={{4,0},{5,1},{6,2},{7,3},{8,12},{9,13},{10,14},{11,15},{20,16},{21,... | collective-permute-start | bytes 1327112 | tf_op jit(solution)/shard_map/ppermute | solution.py:1298
  471.3 4.5 collective-permute-start.56
  472.9 14.1 %collective-permute-start.59 = (bf16[3,192,512]{2,1,0:T(8,128)(2,1)S(1)}, bf16[3,192,512]{2,1,0:T(8,128)(2,1)S(1)}, u32[]{:S(2)}, u32[]{:S(2)}) collective-permute-start(bf16[3,192,512]{2,1,0:T(8,128)(2,1)S(1)} %broadcast_select_fusion.refs_5_.p00), channel_id=1, source_target_pairs={{0,1},{1,0},{2,3},{3,2},{4,5},{5,4},{6,7},{7,6},{8,9},{9,8},{10,11... | collective-permute-start | bytes 1769480 | tf_op jit(solution)/shard_map/ppermute | solution.py:1272
  473.0 14.1 %collective-permute-start.60 = (bf16[3,192,512]{2,1,0:T(8,128)(2,1)S(1)}, bf16[3,192,512]{2,1,0:T(8,128)(2,1)S(1)}, u32[]{:S(2)}, u32[]{:S(2)}) collective-permute-start(bf16[3,192,512]{2,1,0:T(8,128)(2,1)S(1)} %collective-permute-done.48.refs_3_.p01), channel_id=1, source_target_pairs={{0,1},{1,0},{2,3},{3,2},{4,5},{5,4},{6,7},{7,6},{8,9},{9,8},{10,11... | collective-permute-start | bytes 1769480 | tf_op jit(solution)/shard_map/ppermute | solution.py:1272
  473.5 3.8 collective-permute-start.61
  475.9 9.2 %collective-permute-start.57 = (bf16[96,768]{1,0:T(8,128)(2,1)S(1)}, bf16[96,768]{1,0:T(8,128)(2,1)S(1)}, u32[]{:S(2)}, u32[]{:S(2)}) collective-permute-start(bf16[96,768]{1,0:T(8,128)(2,1)S(1)} %add_convert_fusion.14.refs_5_), channel_id=1, source_target_pairs={{4,8},{5,9},{6,10},{7,11},{8,4},{9,5},{10,6},{11,7},{20,24},{21,25... | collective-permute-start | bytes 442376 | tf_op jit(solution)/shard_map/ppermute | solution.py:1298
  477.3 7.8 %collective-permute-start.62 = (f32[8,768]{1,0:T(8,128)S(1)}, f32[8,768]{1,0:T(8,128)S(1)}, u32[]{:S(2)}, u32[]{:S(2)}) collective-permute-start(f32[8,768]{1,0:T(8,128)S(1)} %add.264.refs_6_), channel_id=1, source_target_pairs={{0,8},{1,9},{2,10},{3,11},{4,12},{5,13},{6,14},{7,15},{8,0},{9,1},... | collective-permute-start | bytes 73736 | tf_op jit(solution)/shard_map/ppermute | solution.py:1272
  485.1 7.6 %collective-permute-start.58 = (bf16[96,768]{1,0:T(8,128)(2,1)S(1)}, bf16[96,768]{1,0:T(8,128)(2,1)S(1)}, u32[]{:S(2)}, u32[]{:S(2)}) collective-permute-start(bf16[96,768]{1,0:T(8,128)(2,1)S(1)} %add_convert_fusion.13), channel_id=1, source_target_pairs={{4,0},{5,1},{6,2},{7,3},{8,12},{9,13},{10,14},{11,15},{20,16},{21,... | collective-permute-start | bytes 442376 | tf_op jit(solution)/shard_map/ppermute | solution.py:1298
  (92 other events, 804.5 us)
Sparse Core Ops, SparseCore 0:
  361.8 25.8 all-gather.3
  400.9 26.6 all-gather.5
  471.5 18.5 all-gather.7
